TPU v7x, 256 devices: a whole 4x4x8 slice. The times are simulated.
256 devices in a mesh: scen: 2 (over core), tx: 8 (over y, x_lo), ty: 16 (over x_hi, z).
Axes of the slice: x: 4 (x_hi: 2, x_lo: 2; x = x_hi * 2 + x_lo), y: 4, z: 8, core: 2. Of those that a mesh axis runs over, the one named last changes fastest.
Arguments:
- conductivity: float32 [512, 512, 128], P('tx', 'ty'), may hold values from 0.1 to 1
- cooling: float32 [2, 512, 512, 128], P('scen', 'tx', 'ty'), may hold values from 0.2 to 1.5
- source: float32 [2, 512, 512, 128], P('scen', 'tx', 'ty'), may hold values from -6 to 6
- adjoint_in: float32 [2, 512, 512, 128], P('scen', 'tx', 'ty'), may hold values from -6 to 6
- store: float32 [2, 6, 128, 128, 2048], P('scen', None, ('tx', 'ty')), may hold values from -6 to 6
- holder: int32 [128, 128], P(('tx', 'ty')), may hold values from 0 to 127, each once within a row
- step_index: int32 [2], P('scen'), may hold values from 0 to 5
Outputs:
- adjoint_out: float32 [2, 512, 512, 128], P('scen', 'tx', 'ty')
- grad_conductivity: float32 [512, 512, 128], P('tx', 'ty')
Inputs may be any that keep to these rules, and one draw needn't show every extreme that they name: Each row of holder names each of the 128 devices of tx+ty exactly once.
All inputs are finite; a program needn't handle non-finite values.
Results may differ from a plain program's by a relative error of at most 0.00002.
Values sent between devices are 32-bit elements; how exact they have to be, the bound alone decides.
A program may use at most 64 MiB of HBM per device.

v0:
```python
import jax
import jax.numpy as jnp
from jax import lax
from jax.sharding import PartitionSpec as P

step_size = 0.12


def padded_2(block, sides, width):
    for axis, dim in sides:
        count = lax.axis_size(axis)
        forward = [(i, i + 1) for i in range(count - 1)]
        backward = [(target, source) for source, target in forward]
        low = lax.ppermute(
            lax.slice_in_dim(block, block.shape[dim] - width, None, axis=dim), axis, forward
        )
        high = lax.ppermute(lax.slice_in_dim(block, 0, width, axis=dim), axis, backward)
        block = jnp.concatenate([low, block, high], axis=dim)
    return block


def flux_total(padded, cond_pad):
    face_x = (
        (cond_pad[1:, 1:-1] + cond_pad[:-1, 1:-1]) * 0.5 * (padded[1:, 1:-1] - padded[:-1, 1:-1])
    )
    total = face_x[1:] - face_x[:-1]
    face_y = (
        (cond_pad[1:-1, 1:] + cond_pad[1:-1, :-1]) * 0.5 * (padded[1:-1, 1:] - padded[1:-1, :-1])
    )
    total = total + face_y[:, 1:] - face_y[:, :-1]
    inner_field = padded[1:-1, 1:-1]
    inner_cond = cond_pad[1:-1, 1:-1]
    face_z = (
        (inner_cond[:, :, 1:] + inner_cond[:, :, :-1])
        * 0.5
        * (inner_field[:, :, 1:] - inner_field[:, :, :-1])
    )
    zero_pad = ((0, 0), (0, 0), (0, 1))
    left_pad = ((0, 0), (0, 0), (1, 0))
    return total + jnp.pad(face_z, zero_pad) - jnp.pad(face_z, left_pad)


def face_products(state_pad, adjoint_pad):
    prod_x = (state_pad[1:, 1:-1] - state_pad[:-1, 1:-1]) * (
        adjoint_pad[1:, 1:-1] - adjoint_pad[:-1, 1:-1]
    )
    total = prod_x[1:] + prod_x[:-1]
    prod_y = (state_pad[1:-1, 1:] - state_pad[1:-1, :-1]) * (
        adjoint_pad[1:-1, 1:] - adjoint_pad[1:-1, :-1]
    )
    total = total + prod_y[:, 1:] + prod_y[:, :-1]
    inner_state = state_pad[1:-1, 1:-1]
    inner_adjoint = adjoint_pad[1:-1, 1:-1]
    prod_z = (inner_state[:, :, 1:] - inner_state[:, :, :-1]) * (
        inner_adjoint[:, :, 1:] - inner_adjoint[:, :, :-1]
    )
    zero_pad = ((0, 0), (0, 0), (0, 1))
    left_pad = ((0, 0), (0, 0), (1, 0))
    total = total + jnp.pad(prod_z, zero_pad) + jnp.pad(prod_z, left_pad)
    return -0.5 * step_size * total


def state_halo(field):
    return padded_2(field, (("tx", 0), ("ty", 1)), 1)


def local(conductivity, cooling, source, adjoint_in, store, holder, step_index):
    cells_x, cells_y, cells_z = conductivity.shape
    chosen = lax.dynamic_index_in_dim(store[0, :, 0], step_index[0], 0, keepdims=False)
    arrived = lax.all_to_all(chosen, ("tx", "ty"), split_axis=0, concat_axis=0, tiled=True)
    state_zero = jnp.take(arrived, holder[0], axis=0).reshape(cells_x, cells_y, cells_z)
    cool_here = cooling[0]
    heat_here = source[0]
    adjoint_late = adjoint_in[0]
    near_coeffs = padded_2(jnp.stack([conductivity, adjoint_late]), (("tx", 1), ("ty", 2)), 1)
    cond_near = near_coeffs[0]
    late_near = near_coeffs[1]
    state_near = state_halo(state_zero)
    second_state = state_zero + step_size * (
        flux_total(state_near, cond_near) - cool_here * state_zero + heat_here
    )
    second_near = state_halo(second_state)
    middle_adjoint = adjoint_late + step_size * (
        flux_total(late_near, cond_near) - cool_here * adjoint_late
    )
    middle_near = state_halo(middle_adjoint)
    middle_inner = middle_near[1:-1, 1:-1]
    gradient = face_products(second_near, late_near) + face_products(state_near, middle_near)
    earliest = middle_inner + step_size * (
        flux_total(middle_near, cond_near) - cool_here * middle_inner
    )
    summed = lax.psum(gradient, "scen")
    return (earliest[None], summed)


def solution(mesh):
    in_specs = (
        P("tx", "ty", None),
        P("scen", "tx", "ty", None),
        P("scen", "tx", "ty", None),
        P("scen", "tx", "ty", None),
        P("scen", None, ("tx", "ty"), None, None),
        P(("tx", "ty"), None),
        P("scen"),
    )
    out_specs = (P("scen", "tx", "ty", None), P("tx", "ty", None))
    return jax.shard_map(local, mesh=mesh, in_specs=in_specs, out_specs=out_specs, check_vma=False)
```

profile of v0, /device:TPU:7, one launch (start us, length us, event | category | flops | bytes accessed | tf_op | source)
XLA Modules:
  0.0 167.7 jit_solution(16600107498923234903)
XLA Ops:
  10.8 15.4 %all-to-all-start = ((f32[128,1,2048]{2,1,0:T(1,128)}), f32[128,1,2048]{2,1,0:T(1,128)}, u32[]{:S(2)}, u32[]{:S(2)}) async-start(f32[128,1,2048]{2,1,0:T(1,128)} %all_to_all.8), calls=%async_computation | async-start | bytes 2097152 | tf_op jit(solution)/shard_map/all_to_all | solution.py:70
  26.4 3.5 %collective-permute-start = (f32[2,1,32,128]{3,2,1,0:T(8,128)S(1)}, f32[2,1,32,128]{3,2,1,0:T(8,128)S(1)}, u32[]{:S(2)}, u32[]{:S(2)}) collective-permute-start(f32[2,1,32,128]{3,2,1,0:T(8,128)S(1)} %get-tuple-element.6), channel_id=1, source_target_pairs={{0,16},{16,32},{32,48},{48,64},{64,80},{80,96},{96,112},{1,17},{17... | collective-permute-start | bytes 98312 | tf_op jit(solution)/shard_map/ppermute | solution.py:14
  29.9 1.9 %collective-permute-start.1 = (f32[2,1,32,128]{3,2,1,0:T(8,128)S(1)}, f32[2,1,32,128]{3,2,1,0:T(8,128)S(1)}, u32[]{:S(2)}, u32[]{:S(2)}) collective-permute-start(f32[2,1,32,128]{3,2,1,0:T(8,128)S(1)} %get-tuple-element.7), channel_id=1, source_target_pairs={{16,0},{32,16},{48,32},{64,48},{80,64},{96,80},{112,96},{17,1},{33... | collective-permute-start | bytes 98312 | tf_op jit(solution)/shard_map/ppermute | solution.py:17
  33.4 2.6 %collective-permute-done.1 = f32[2,1,32,128]{3,2,1,0:T(8,128)S(1)} collective-permute-done((f32[2,1,32,128]{3,2,1,0:T(8,128)S(1)}, f32[2,1,32,128]{3,2,1,0:T(8,128)S(1)}, u32[]{:S(2)}, u32[]{:S(2)}) %collective-permute-start.1) | collective-permute-done | bytes 32800 | tf_op jit(solution)/shard_map/ppermute | solution.py:17
  36.0 3.2 %collective-permute-start.2 = (f32[2,66,1,128]{3,2,1,0:T(1,128)S(1)}, f32[2,66,1,128]{3,2,1,0:T(1,128)S(1)}, u32[]{:S(2)}, u32[]{:S(2)}) collective-permute-start(f32[2,66,1,128]{3,2,1,0:T(1,128)S(1)} %get-tuple-element.4), channel_id=1, source_target_pairs={{0,1},{1,2},{2,3},{3,4},{4,5},{5,6},{6,7},{7,8},{8,9},{9,10},{10,1... | collective-permute-start | bytes 202760 | tf_op jit(solution)/shard_map/ppermute | solution.py:14
  39.2 5.7 %collective-permute-start.3 = (f32[2,66,1,128]{3,2,1,0:T(1,128)S(1)}, f32[2,66,1,128]{3,2,1,0:T(1,128)S(1)}, u32[]{:S(2)}, u32[]{:S(2)}) collective-permute-start(f32[2,66,1,128]{3,2,1,0:T(1,128)S(1)} %get-tuple-element.5), channel_id=1, source_target_pairs={{1,0},{2,1},{3,2},{4,3},{5,4},{6,5},{7,6},{8,7},{9,8},{10,9},{11,1... | collective-permute-start | bytes 202760 | tf_op jit(solution)/shard_map/ppermute | solution.py:17
  45.0 6.0 %collective-permute-done.2 = f32[2,66,1,128]{3,2,1,0:T(1,128)S(1)} collective-permute-done((f32[2,66,1,128]{3,2,1,0:T(1,128)S(1)}, f32[2,66,1,128]{3,2,1,0:T(1,128)S(1)}, u32[]{:S(2)}, u32[]{:S(2)}) %collective-permute-start.2) | collective-permute-done | bytes 67616 | tf_op jit(solution)/shard_map/ppermute | solution.py:14
  56.4 2.4 %gather.7 = f32[64,32,128]{2,1,0:T(8,128)} reshape(f32[128,2048]{1,0:T(8,128)} %gather_fusion) | data formatting | bytes 2097152 | tf_op jit(solution)/shard_map/jit(_take)/gather | solution.py:71
  59.1 1.9 %collective-permute-start.8 = (f32[1,32,128]{2,1,0:T(8,128)S(1)}, f32[1,32,128]{2,1,0:T(8,128)S(1)}, u32[]{:S(2)}, u32[]{:S(2)}) collective-permute-start(f32[1,32,128]{2,1,0:T(8,128)S(1)} %slice.284), channel_id=1, source_target_pairs={{16,0},{32,16},{48,32},{64,48},{80,64},{96,80},{112,96},{17,1},{33... | collective-permute-start | bytes 49160 | tf_op jit(solution)/shard_map/ppermute | solution.py:17
  61.0 4.3 %collective-permute-start.9 = (f32[1,32,128]{2,1,0:T(8,128)S(1)}, f32[1,32,128]{2,1,0:T(8,128)S(1)}, u32[]{:S(2)}, u32[]{:S(2)}) collective-permute-start(f32[1,32,128]{2,1,0:T(8,128)S(1)} %slice.286), channel_id=1, source_target_pairs={{0,16},{16,32},{32,48},{48,64},{64,80},{80,96},{96,112},{1,17},{17... | collective-permute-start | bytes 49160 | tf_op jit(solution)/shard_map/ppermute | solution.py:14
  67.6 4.5 %collective-permute-start.10 = (f32[66,1,128]{2,1,0:T(1,128)S(1)}, f32[66,1,128]{2,1,0:T(1,128)S(1)}, u32[]{:S(2)}, u32[]{:S(2)}) collective-permute-start(f32[66,1,128]{2,1,0:T(1,128)S(1)} %get-tuple-element.18), channel_id=1, source_target_pairs={{1,0},{2,1},{3,2},{4,3},{5,4},{6,5},{7,6},{8,7},{9,8},{10,9},{11,1... | collective-permute-start | bytes 101384 | tf_op jit(solution)/shard_map/ppermute | solution.py:17
  72.1 1.9 %collective-permute-start.11 = (f32[66,1,128]{2,1,0:T(1,128)S(1)}, f32[66,1,128]{2,1,0:T(1,128)S(1)}, u32[]{:S(2)}, u32[]{:S(2)}) collective-permute-start(f32[66,1,128]{2,1,0:T(1,128)S(1)} %get-tuple-element.19), channel_id=1, source_target_pairs={{0,1},{1,2},{2,3},{3,4},{4,5},{5,6},{6,7},{7,8},{8,9},{9,10},{10,1... | collective-permute-start | bytes 101384 | tf_op jit(solution)/shard_map/ppermute | solution.py:14
  74.3 6.0 %collective-permute-done.11 = f32[66,1,128]{2,1,0:T(1,128)S(1)} collective-permute-done((f32[66,1,128]{2,1,0:T(1,128)S(1)}, f32[66,1,128]{2,1,0:T(1,128)S(1)}, u32[]{:S(2)}, u32[]{:S(2)}) %collective-permute-start.11) | collective-permute-done | bytes 33824 | tf_op jit(solution)/shard_map/ppermute | solution.py:14
  83.8 4.3 %collective-permute-start.13 = (f32[1,32,128]{2,1,0:T(8,128)S(1)}, f32[1,32,128]{2,1,0:T(8,128)S(1)}, u32[]{:S(2)}, u32[]{:S(2)}) collective-permute-start(f32[1,32,128]{2,1,0:T(8,128)S(1)} %get-tuple-element.24), channel_id=1, source_target_pairs={{0,16},{16,32},{32,48},{48,64},{64,80},{80,96},{96,112},{1,17},{17... | collective-permute-start | bytes 49160 | tf_op jit(solution)/shard_map/ppermute | solution.py:14
  89.1 2.2 %collective-permute-start.14 = (f32[66,1,128]{2,1,0:T(1,128)S(1)}, f32[66,1,128]{2,1,0:T(1,128)S(1)}, u32[]{:S(2)}, u32[]{:S(2)}) collective-permute-start(f32[66,1,128]{2,1,0:T(1,128)S(1)} %get-tuple-element.14), channel_id=1, source_target_pairs={{1,0},{2,1},{3,2},{4,3},{5,4},{6,5},{7,6},{8,7},{9,8},{10,9},{11,1... | collective-permute-start | bytes 101384 | tf_op jit(solution)/shard_map/ppermute | solution.py:17
  91.4 3.1 %collective-permute-start.15 = (f32[66,1,128]{2,1,0:T(1,128)S(1)}, f32[66,1,128]{2,1,0:T(1,128)S(1)}, u32[]{:S(2)}, u32[]{:S(2)}) collective-permute-start(f32[66,1,128]{2,1,0:T(1,128)S(1)} %get-tuple-element.15), channel_id=1, source_target_pairs={{0,1},{1,2},{2,3},{3,4},{4,5},{5,6},{6,7},{7,8},{8,9},{9,10},{10,1... | collective-permute-start | bytes 101384 | tf_op jit(solution)/shard_map/ppermute | solution.py:14
  94.9 4.7 %collective-permute-done.15 = f32[66,1,128]{2,1,0:T(1,128)S(1)} collective-permute-done((f32[66,1,128]{2,1,0:T(1,128)S(1)}, f32[66,1,128]{2,1,0:T(1,128)S(1)}, u32[]{:S(2)}, u32[]{:S(2)}) %collective-permute-start.15) | collective-permute-done | bytes 33824 | tf_op jit(solution)/shard_map/ppermute | solution.py:14
  103.2 4.3 %collective-permute-start.5 = (f32[1,32,128]{2,1,0:T(8,128)S(1)}, f32[1,32,128]{2,1,0:T(8,128)S(1)}, u32[]{:S(2)}, u32[]{:S(2)}) collective-permute-start(f32[1,32,128]{2,1,0:T(8,128)S(1)} %get-tuple-element.28), channel_id=1, source_target_pairs={{0,16},{16,32},{32,48},{48,64},{64,80},{80,96},{96,112},{1,17},{17... | collective-permute-start | bytes 49160 | tf_op jit(solution)/shard_map/ppermute | solution.py:14
  107.4 1.9 %fusion.38 = (f32[64,32,127]{2,1,0:T(8,128)S(1)}, f32[64,32,127]{2,1,0:T(8,128)}) fusion(f32[64,32,128]{2,1,0:T(8,128)S(1)} %fusion.31, f32[64,32,128]{2,1,0:T(8,128)S(1)} %broadcast_select_fusion.1, f32[66,34,128]{2,1,0:T(8,128)S(1)} %get-tuple-element.2), kind=kLoop, calls=%fused_computation.93 | loop fusion | flops 1560576 | bytes 8323072 | tf_op jit(solution)/shard_map/mul | solution.py:54
  109.4 2.0 %collective-permute-start.6 = (f32[66,1,128]{2,1,0:T(1,128)S(1)}, f32[66,1,128]{2,1,0:T(1,128)S(1)}, u32[]{:S(2)}, u32[]{:S(2)}) collective-permute-start(f32[66,1,128]{2,1,0:T(1,128)S(1)} %get-tuple-element.20), channel_id=1, source_target_pairs={{1,0},{2,1},{3,2},{4,3},{5,4},{6,5},{7,6},{8,7},{9,8},{10,9},{11,1... | collective-permute-start | bytes 101384 | tf_op jit(solution)/shard_map/ppermute | solution.py:17
  111.4 3.4 %collective-permute-start.7 = (f32[66,1,128]{2,1,0:T(1,128)S(1)}, f32[66,1,128]{2,1,0:T(1,128)S(1)}, u32[]{:S(2)}, u32[]{:S(2)}) collective-permute-start(f32[66,1,128]{2,1,0:T(1,128)S(1)} %get-tuple-element.21), channel_id=1, source_target_pairs={{0,1},{1,2},{2,3},{3,4},{4,5},{5,6},{6,7},{7,8},{8,9},{9,10},{10,1... | collective-permute-start | bytes 101384 | tf_op jit(solution)/shard_map/ppermute | solution.py:14
  116.3 3.4 %collective-permute-done.7 = f32[66,1,128]{2,1,0:T(1,128)S(1)} collective-permute-done((f32[66,1,128]{2,1,0:T(1,128)S(1)}, f32[66,1,128]{2,1,0:T(1,128)S(1)}, u32[]{:S(2)}, u32[]{:S(2)}) %collective-permute-start.7) | collective-permute-done | bytes 33824 | tf_op jit(solution)/shard_map/ppermute | solution.py:14
  125.7 33.0 %all-reduce.12.cloned.1.call-done = f32[64,32,128]{2,1,0:T(8,128)} async-done(((f32[64,32,128]{2,1,0:T(8,128)}), f32[64,32,128]{2,1,0:T(8,128)}) %all-reduce.12.cloned.1.call-update) | async-done | bytes 1048592 | tf_op jit(solution)/shard_map/psum | solution.py:92
  158.6 2.3 %copy.18 = f32[64,32,128]{2,1,0:T(8,128)} copy(f32[64,32,128]{2,1,0:T(8,128)} %all-reduce.12.cloned.1.call-done) | data formatting | bytes 2097152
  (79 shorter events, 28.6 us)
Async XLA Ops:
  10.8 15.5 %copy-start.1 = (f32[1,64,32,128]{3,2,1,0:T(8,128)S(1)}, f32[1,64,32,128]{3,2,1,0:T(8,128)}, u32[]{:S(2)}) copy-start(f32[1,64,32,128]{3,2,1,0:T(8,128)} %param.10) | copy-start | bytes 3145732
  10.8 15.5 %copy-start.3 = (f32[64,32,128]{2,1,0:T(8,128)S(1)}, f32[64,32,128]{2,1,0:T(8,128)}, u32[]{:S(2)}) copy-start(f32[64,32,128]{2,1,0:T(8,128)} %param.7) | copy-start | bytes 3145732
  10.8 42.1 %all-to-all-start = ((f32[128,1,2048]{2,1,0:T(1,128)}), f32[128,1,2048]{2,1,0:T(1,128)}, u32[]{:S(2)}, u32[]{:S(2)}) async-start(f32[128,1,2048]{2,1,0:T(1,128)} %all_to_all.8), calls=%async_computation | async-start | bytes 2097152 | tf_op jit(solution)/shard_map/all_to_all | solution.py:70
  26.3 132.3 %all-reduce.12.cloned.1.call-start = ((), (), s32[]{:S(2)}) async-start(), calls=%async_computation.1 | async-start | bytes 2097152 | tf_op jit(solution)/shard_map/psum | solution.py:92
  26.4 7.0 %collective-permute-start = (f32[2,1,32,128]{3,2,1,0:T(8,128)S(1)}, f32[2,1,32,128]{3,2,1,0:T(8,128)S(1)}, u32[]{:S(2)}, u32[]{:S(2)}) collective-permute-start(f32[2,1,32,128]{3,2,1,0:T(8,128)S(1)} %get-tuple-element.6), channel_id=1, source_target_pairs={{0,16},{16,32},{32,48},{48,64},{64,80},{80,96},{96,112},{1,17},{17... | collective-permute-start | bytes 98312 | tf_op jit(solution)/shard_map/ppermute | solution.py:14
  29.9 6.1 %collective-permute-start.1 = (f32[2,1,32,128]{3,2,1,0:T(8,128)S(1)}, f32[2,1,32,128]{3,2,1,0:T(8,128)S(1)}, u32[]{:S(2)}, u32[]{:S(2)}) collective-permute-start(f32[2,1,32,128]{3,2,1,0:T(8,128)S(1)} %get-tuple-element.7), channel_id=1, source_target_pairs={{16,0},{32,16},{48,32},{64,48},{80,64},{96,80},{112,96},{17,1},{33... | collective-permute-start | bytes 98312 | tf_op jit(solution)/shard_map/ppermute | solution.py:17
  36.0 14.9 %collective-permute-start.2 = (f32[2,66,1,128]{3,2,1,0:T(1,128)S(1)}, f32[2,66,1,128]{3,2,1,0:T(1,128)S(1)}, u32[]{:S(2)}, u32[]{:S(2)}) collective-permute-start(f32[2,66,1,128]{3,2,1,0:T(1,128)S(1)} %get-tuple-element.4), channel_id=1, source_target_pairs={{0,1},{1,2},{2,3},{3,4},{4,5},{5,6},{6,7},{7,8},{8,9},{9,10},{10,1... | collective-permute-start | bytes 202760 | tf_op jit(solution)/shard_map/ppermute | solution.py:14
  39.2 11.8 %collective-permute-start.3 = (f32[2,66,1,128]{3,2,1,0:T(1,128)S(1)}, f32[2,66,1,128]{3,2,1,0:T(1,128)S(1)}, u32[]{:S(2)}, u32[]{:S(2)}) collective-permute-start(f32[2,66,1,128]{3,2,1,0:T(1,128)S(1)} %get-tuple-element.5), channel_id=1, source_target_pairs={{1,0},{2,1},{3,2},{4,3},{5,4},{6,5},{7,6},{8,7},{9,8},{10,9},{11,1... | collective-permute-start | bytes 202760 | tf_op jit(solution)/shard_map/ppermute | solution.py:17
  59.1 8.5 %collective-permute-start.8 = (f32[1,32,128]{2,1,0:T(8,128)S(1)}, f32[1,32,128]{2,1,0:T(8,128)S(1)}, u32[]{:S(2)}, u32[]{:S(2)}) collective-permute-start(f32[1,32,128]{2,1,0:T(8,128)S(1)} %slice.284), channel_id=1, source_target_pairs={{16,0},{32,16},{48,32},{64,48},{80,64},{96,80},{112,96},{17,1},{33... | collective-permute-start | bytes 49160 | tf_op jit(solution)/shard_map/ppermute | solution.py:17
  61.0 6.5 %collective-permute-start.9 = (f32[1,32,128]{2,1,0:T(8,128)S(1)}, f32[1,32,128]{2,1,0:T(8,128)S(1)}, u32[]{:S(2)}, u32[]{:S(2)}) collective-permute-start(f32[1,32,128]{2,1,0:T(8,128)S(1)} %slice.286), channel_id=1, source_target_pairs={{0,16},{16,32},{32,48},{48,64},{64,80},{80,96},{96,112},{1,17},{17... | collective-permute-start | bytes 49160 | tf_op jit(solution)/shard_map/ppermute | solution.py:14
  67.6 6.7 %collective-permute-start.10 = (f32[66,1,128]{2,1,0:T(1,128)S(1)}, f32[66,1,128]{2,1,0:T(1,128)S(1)}, u32[]{:S(2)}, u32[]{:S(2)}) collective-permute-start(f32[66,1,128]{2,1,0:T(1,128)S(1)} %get-tuple-element.18), channel_id=1, source_target_pairs={{1,0},{2,1},{3,2},{4,3},{5,4},{6,5},{7,6},{8,7},{9,8},{10,9},{11,1... | collective-permute-start | bytes 101384 | tf_op jit(solution)/shard_map/ppermute | solution.py:17
  72.1 8.3 %collective-permute-start.11 = (f32[66,1,128]{2,1,0:T(1,128)S(1)}, f32[66,1,128]{2,1,0:T(1,128)S(1)}, u32[]{:S(2)}, u32[]{:S(2)}) collective-permute-start(f32[66,1,128]{2,1,0:T(1,128)S(1)} %get-tuple-element.19), channel_id=1, source_target_pairs={{0,1},{1,2},{2,3},{3,4},{4,5},{5,6},{6,7},{7,8},{8,9},{9,10},{10,1... | collective-permute-start | bytes 101384 | tf_op jit(solution)/shard_map/ppermute | solution.py:14
  74.3 6.6 %copy-start.4 = (f32[64,32,128]{2,1,0:T(8,128)S(1)}, f32[64,32,128]{2,1,0:T(8,128)}, u32[]{:S(2)}) copy-start(f32[64,32,128]{2,1,0:T(8,128)} %gather.7) | copy-start | bytes 3145732
  74.3 6.6 %copy-start.5 = (f32[1,64,32,128]{3,2,1,0:T(8,128)S(1)}, f32[1,64,32,128]{3,2,1,0:T(8,128)}, u32[]{:S(2)}) copy-start(f32[1,64,32,128]{3,2,1,0:T(8,128)} %param.8) | copy-start | bytes 3145732
  74.3 6.6 %copy-start.9 = (f32[1,64,32,128]{3,2,1,0:T(8,128)S(1)}, f32[1,64,32,128]{3,2,1,0:T(8,128)}, u32[]{:S(2)}) copy-start(f32[1,64,32,128]{3,2,1,0:T(8,128)} %param.9) | copy-start | bytes 3145732
  80.9 7.2 %copy-start = (f32[66,34,128]{2,1,0:T(8,128)S(1)}, f32[66,34,128]{2,1,0:T(8,128)}, u32[]{:S(2)}) copy-start(f32[66,34,128]{2,1,0:T(8,128)} %get-tuple-element.3) | copy-start | bytes 3446788
  81.9 7.2 %collective-permute-start.12 = (f32[1,32,128]{2,1,0:T(8,128)S(1)}, f32[1,32,128]{2,1,0:T(8,128)S(1)}, u32[]{:S(2)}, u32[]{:S(2)}) collective-permute-start(f32[1,32,128]{2,1,0:T(8,128)S(1)} %get-tuple-element.25), channel_id=1, source_target_pairs={{16,0},{32,16},{48,32},{64,48},{80,64},{96,80},{112,96},{17,1},{33... | collective-permute-start | bytes 49160 | tf_op jit(solution)/shard_map/ppermute | solution.py:17
  83.8 5.3 %collective-permute-start.13 = (f32[1,32,128]{2,1,0:T(8,128)S(1)}, f32[1,32,128]{2,1,0:T(8,128)S(1)}, u32[]{:S(2)}, u32[]{:S(2)}) collective-permute-start(f32[1,32,128]{2,1,0:T(8,128)S(1)} %get-tuple-element.24), channel_id=1, source_target_pairs={{0,16},{16,32},{32,48},{48,64},{64,80},{80,96},{96,112},{1,17},{17... | collective-permute-start | bytes 49160 | tf_op jit(solution)/shard_map/ppermute | solution.py:14
  89.1 5.8 %collective-permute-start.14 = (f32[66,1,128]{2,1,0:T(1,128)S(1)}, f32[66,1,128]{2,1,0:T(1,128)S(1)}, u32[]{:S(2)}, u32[]{:S(2)}) collective-permute-start(f32[66,1,128]{2,1,0:T(1,128)S(1)} %get-tuple-element.14), channel_id=1, source_target_pairs={{1,0},{2,1},{3,2},{4,3},{5,4},{6,5},{7,6},{8,7},{9,8},{10,9},{11,1... | collective-permute-start | bytes 101384 | tf_op jit(solution)/shard_map/ppermute | solution.py:17
  91.4 8.3 %collective-permute-start.15 = (f32[66,1,128]{2,1,0:T(1,128)S(1)}, f32[66,1,128]{2,1,0:T(1,128)S(1)}, u32[]{:S(2)}, u32[]{:S(2)}) collective-permute-start(f32[66,1,128]{2,1,0:T(1,128)S(1)} %get-tuple-element.15), channel_id=1, source_target_pairs={{0,1},{1,2},{2,3},{3,4},{4,5},{5,6},{6,7},{7,8},{8,9},{9,10},{10,1... | collective-permute-start | bytes 101384 | tf_op jit(solution)/shard_map/ppermute | solution.py:14
  101.2 8.1 %collective-permute-start.4 = (f32[1,32,128]{2,1,0:T(8,128)S(1)}, f32[1,32,128]{2,1,0:T(8,128)S(1)}, u32[]{:S(2)}, u32[]{:S(2)}) collective-permute-start(f32[1,32,128]{2,1,0:T(8,128)S(1)} %get-tuple-element.29), channel_id=1, source_target_pairs={{16,0},{32,16},{48,32},{64,48},{80,64},{96,80},{112,96},{17,1},{33... | collective-permute-start | bytes 49160 | tf_op jit(solution)/shard_map/ppermute | solution.py:17
  103.2 6.2 %collective-permute-start.5 = (f32[1,32,128]{2,1,0:T(8,128)S(1)}, f32[1,32,128]{2,1,0:T(8,128)S(1)}, u32[]{:S(2)}, u32[]{:S(2)}) collective-permute-start(f32[1,32,128]{2,1,0:T(8,128)S(1)} %get-tuple-element.28), channel_id=1, source_target_pairs={{0,16},{16,32},{32,48},{48,64},{64,80},{80,96},{96,112},{1,17},{17... | collective-permute-start | bytes 49160 | tf_op jit(solution)/shard_map/ppermute | solution.py:14
  109.4 6.9 %collective-permute-start.6 = (f32[66,1,128]{2,1,0:T(1,128)S(1)}, f32[66,1,128]{2,1,0:T(1,128)S(1)}, u32[]{:S(2)}, u32[]{:S(2)}) collective-permute-start(f32[66,1,128]{2,1,0:T(1,128)S(1)} %get-tuple-element.20), channel_id=1, source_target_pairs={{1,0},{2,1},{3,2},{4,3},{5,4},{6,5},{7,6},{8,7},{9,8},{10,9},{11,1... | collective-permute-start | bytes 101384 | tf_op jit(solution)/shard_map/ppermute | solution.py:17
  111.4 8.3 %collective-permute-start.7 = (f32[66,1,128]{2,1,0:T(1,128)S(1)}, f32[66,1,128]{2,1,0:T(1,128)S(1)}, u32[]{:S(2)}, u32[]{:S(2)}) collective-permute-start(f32[66,1,128]{2,1,0:T(1,128)S(1)} %get-tuple-element.21), channel_id=1, source_target_pairs={{0,1},{1,2},{2,3},{3,4},{4,5},{5,6},{6,7},{7,8},{8,9},{9,10},{10,1... | collective-permute-start | bytes 101384 | tf_op jit(solution)/shard_map/ppermute | solution.py:14
  (5 other events, 13.1 us)
Sparse Core Ops, SparseCore 0:
  122.2 36.3 all-reduce.11
where the time goes:
time: 170 us; the launch traced here: 168 us
  starting transfers between devices  65.5 us (39%)
  waiting for transfers between devices  56 us (33%)
  other arithmetic  16.3 us (10%)
  between operations  15.2 us (9%)
  local copies, waits for them, and re-layouts  14.8 us (9%)
    psum x1, waiting for transfers between devices, local(): summed = lax.psum(gradient, 'scen')  33 us
    ppermute x8, starting transfers between devices, padded_2(): lax.ppermute(lax.slice_in_dim(block, block.shape[dim] - width, None, axis...  27.9 us
    ppermute x8, starting transfers between devices, padded_2(): lax.ppermute(lax.slice_in_dim(block, 0, width, axis=dim), axis, backward)  22.1 us
    ppermute x8, waiting for transfers between devices, padded_2(): lax.ppermute(lax.slice_in_dim(block, block.shape[dim] - width, None, axis...  20.2 us
    all_to_all x1, starting transfers between devices, local(): lax.all_to_all(chosen, ('tx', 'ty'), split_axis=0, concat_axis=0, tiled=T...  15.4 us
    unnamed x25, local copies, waits for them, and re-layouts  5.75 us
    gather x2, local copies, waits for them, and re-layouts, local(): jnp.take(arrived, holder[0], axis=0).reshape(cells_x, cells_y, cells_z)  4.36 us
  transfers between devices with their start and end apart: 18, of which 7 were waited for; matrix products, arithmetic and copies ran while one was open for 8% of the time, Pallas kernels for 0%

commit v1 on v0

--- a/solution.py
+++ b/solution.py
@@ -1,9 +1,81 @@
+import functools
+
 import jax
 import jax.numpy as jnp
 from jax import lax
+from jax.experimental import pallas as pl
+from jax.experimental.pallas import tpu as pltpu
 from jax.sharding import PartitionSpec as P
 
+MESH = pl.DeviceIdType.MESH
 step_size = 0.12
+
+
+def exchange_kernel(n_ty, tiles, src, dst, send_sem, recv_sem, local_sem):
+    scen = lax.axis_index("scen")
+    me = lax.axis_index("tx") * n_ty + lax.axis_index("ty")
+
+    def device(k):
+        t = (me + k) % tiles
+        return t, (scen, t // n_ty, t % n_ty)
+
+    barrier = pltpu.get_barrier_semaphore()
+
+    def greet(k, carry):
+        pl.semaphore_signal(barrier, inc=1, device_id=device(k)[1], device_id_type=MESH)
+        return carry
+
+    lax.fori_loop(1, tiles, greet, 0)
+    pl.semaphore_wait(barrier, tiles - 1)
+    own = pltpu.make_async_copy(src.at[me], dst.at[me], local_sem)
+    own.start()
+
+    def send(k, carry):
+        t, target = device(k)
+        pltpu.make_async_remote_copy(
+            src_ref=src.at[t],
+            dst_ref=dst.at[me],
+            send_sem=send_sem,
+            recv_sem=recv_sem,
+            device_id=target,
+            device_id_type=MESH,
+        ).start()
+        return carry
+
+    lax.fori_loop(1, tiles, send, 0)
+    own.wait()
+    others = pl.ds(0, tiles - 1)
+    pltpu.make_async_copy(src.at[others], src.at[others], send_sem).wait()
+    pltpu.make_async_copy(dst.at[others], dst.at[others], recv_sem).wait()
+
+
+def exchange(pieces, n_ty):
+    tiles = pieces.shape[0]
+    return pl.pallas_call(
+        functools.partial(exchange_kernel, n_ty, tiles),
+        out_shape=jax.ShapeDtypeStruct(pieces.shape, pieces.dtype),
+        in_specs=[pl.BlockSpec(memory_space=pltpu.VMEM)],
+        out_specs=pl.BlockSpec(memory_space=pltpu.VMEM),
+        scratch_shapes=[pltpu.SemaphoreType.DMA] * 3,
+        compiler_params=pltpu.CompilerParams(collective_id=0, has_side_effects=True),
+    )(pieces)
+
+
+def assemble_kernel(holder, arrived, state):
+    def place(j, carry):
+        state[j] = arrived[holder[j]]
+        return carry
+
+    lax.fori_loop(0, state.shape[0], place, 0, unroll=8)
+
+
+def assemble(arrived, holder):
+    return pl.pallas_call(
+        assemble_kernel,
+        out_shape=jax.ShapeDtypeStruct(arrived.shape, arrived.dtype),
+        in_specs=[pl.BlockSpec(memory_space=pltpu.SMEM), pl.BlockSpec(memory_space=pltpu.VMEM)],
+        out_specs=pl.BlockSpec(memory_space=pltpu.VMEM),
+    )(holder, arrived)
 
 
 def padded_2(block, sides, width):
@@ -67,8 +139,8 @@
 def local(conductivity, cooling, source, adjoint_in, store, holder, step_index):
     cells_x, cells_y, cells_z = conductivity.shape
     chosen = lax.dynamic_index_in_dim(store[0, :, 0], step_index[0], 0, keepdims=False)
-    arrived = lax.all_to_all(chosen, ("tx", "ty"), split_axis=0, concat_axis=0, tiled=True)
-    state_zero = jnp.take(arrived, holder[0], axis=0).reshape(cells_x, cells_y, cells_z)
+    arrived = exchange(chosen.reshape(chosen.shape[0], -1, cells_z), lax.axis_size("ty"))
+    state_zero = assemble(arrived, holder[0]).reshape(cells_x, cells_y, cells_z)
     cool_here = cooling[0]
     heat_here = source[0]
     adjoint_late = adjoint_in[0]
@@ -89,7 +161,7 @@
     earliest = middle_inner + step_size * (
         flux_total(middle_near, cond_near) - cool_here * middle_inner
     )
-    summed = lax.psum(gradient, "scen")
+    summed = gradient + lax.ppermute(gradient, "scen", [(0, 1), (1, 0)])
     return (earliest[None], summed)
 
 

time: 170 us -> 132 us (0.78)
  waiting for transfers between devices: 56 us -> 14.2 us
  Pallas kernels: 0 us -> 39.9 us
  between operations: 15.2 us -> 1.71 us
  local copies, waits for them, and re-layouts: 14.8 us -> 3.52 us
  starting transfers between devices: 65.5 us -> 57.8 us
  other arithmetic: 16.3 us -> 12.7 us
    pallas_call x0 -> x2, Pallas kernels: none -> 39.9 us  [the longest x1 37.3 us: exchange(): pl.pallas_call(functools.partial(exchange_kernel, n_ty, tiles), out_shape...]
    psum x1 -> x0, waiting for transfers between devices: 33 us -> none  [local(): summed = lax.psum(gradient, 'scen')]
    all_to_all x1 -> x0, starting transfers between devices: 15.4 us -> none  [local(): lax.all_to_all(chosen, ('tx', 'ty'), split_axis=0, concat_axis=0, tiled=T...]
    ppermute x0 -> x1, starting transfers between devices: none -> 9.11 us  [local(): summed = gradient + lax.ppermute(gradient, 'scen', [(0, 1), (1, 0)])]
    ppermute x8, waiting for transfers between devices: 20.2 us -> 14 us  [padded_2(): lax.ppermute(lax.slice_in_dim(block, block.shape[dim] - width, None, axis...]
    gather x2 -> x0, local copies, waits for them, and re-layouts: 4.36 us -> none  [local(): jnp.take(arrived, holder[0], axis=0).reshape(cells_x, cells_y, cells_z)]
    unnamed x25 -> x12, local copies, waits for them, and re-layouts: 5.75 us -> 2.51 us
    ppermute x8, waiting for transfers between devices: 2.58 us -> 0.02 us  [padded_2(): lax.ppermute(lax.slice_in_dim(block, 0, width, axis=dim), axis, backward)]
  transfers between devices with their start and end apart: 18 -> 17, of which waited for: 7 -> 4; matrix products, arithmetic and copies ran while one was open for 8% -> 8% of each run, Pallas kernels for 0% -> 31%
where the time goes in v1:
time: 132 us; the launch traced here: 130 us
  starting transfers between devices  57.8 us (44%)
  Pallas kernels  39.9 us (30%)
  waiting for transfers between devices  14.2 us (11%)
  other arithmetic  12.7 us (10%)
  local copies, waits for them, and re-layouts  3.52 us (3%)
  between operations  1.71 us (1%)
    pallas_call x1, Pallas kernels, exchange(): pl.pallas_call(functools.partial(exchange_kernel, n_ty, tiles), out_shape...  37.3 us
    ppermute x8, starting transfers between devices, padded_2(): lax.ppermute(lax.slice_in_dim(block, block.shape[dim] - width, None, axis...  27.3 us
    ppermute x8, starting transfers between devices, padded_2(): lax.ppermute(lax.slice_in_dim(block, 0, width, axis=dim), axis, backward)  21.3 us
    ppermute x8, waiting for transfers between devices, padded_2(): lax.ppermute(lax.slice_in_dim(block, block.shape[dim] - width, None, axis...  14 us
    ppermute x1, starting transfers between devices, local(): summed = gradient + lax.ppermute(gradient, 'scen', [(0, 1), (1, 0)])  9.11 us
  transfers between devices with their start and end apart: 17, of which 4 were waited for; matrix products, arithmetic and copies ran while one was open for 8% of the time, Pallas kernels for 31%

profile of v1, /device:TPU:7, one launch (start us, length us, event | category | flops | bytes accessed | tf_op | source)
XLA Modules:
  0.0 129.7 jit_solution(17283408992496655768)
XLA Ops:
  1.4 3.5 %collective-permute-start = (f32[2,1,32,128]{3,2,1,0:T(8,128)S(1)}, f32[2,1,32,128]{3,2,1,0:T(8,128)S(1)}, u32[]{:S(2)}, u32[]{:S(2)}) collective-permute-start(f32[2,1,32,128]{3,2,1,0:T(8,128)S(1)} %get-tuple-element.6), channel_id=1, source_target_pairs={{0,16},{16,32},{32,48},{48,64},{64,80},{80,96},{96,112},{1,17},{17... | collective-permute-start | bytes 98312 | tf_op jit(solution)/shard_map/ppermute | solution.py:86
  4.9 1.9 %collective-permute-start.1 = (f32[2,1,32,128]{3,2,1,0:T(8,128)S(1)}, f32[2,1,32,128]{3,2,1,0:T(8,128)S(1)}, u32[]{:S(2)}, u32[]{:S(2)}) collective-permute-start(f32[2,1,32,128]{3,2,1,0:T(8,128)S(1)} %get-tuple-element.7), channel_id=1, source_target_pairs={{16,0},{32,16},{48,32},{64,48},{80,64},{96,80},{112,96},{17,1},{33... | collective-permute-start | bytes 98312 | tf_op jit(solution)/shard_map/ppermute | solution.py:89
  7.5 1.3 %dynamic-slice_bitcast_fusion = f32[16,8,16,128]{3,1,2,0:T(8,128)S(1)} fusion(f32[1,6,1,128,2048]{4,3,2,1,0:T(8,128)} %param.11, s32[]{:T(128)S(6)} %select_n.4), kind=kLoop, calls=%fused_computation.83 | loop fusion | bytes 2097156
  9.9 37.3 %shard_map.86.arrived = f32[128,16,128]{2,1,0:T(8,128)} custom-call(f32[128,16,128]{2,1,0:T(8,128)} %bitcast.47), custom_call_target="tpu_custom_call" | custom-call | tf_op jit(solution)/shard_map/pallas_call | solution.py:54
  47.3 2.6 %shard_map.87 = f32[128,16,128]{2,1,0:T(8,128)} custom-call(s32[128]{0:T(128)} %bitcast.50, f32[128,16,128]{2,1,0:T(8,128)} %shard_map.86.arrived), custom_call_target="tpu_custom_call" | custom-call | tf_op jit(solution)/shard_map/pallas_call | solution.py:73
  50.7 1.9 %collective-permute-start.8 = (f32[1,32,128]{2,1,0:T(8,128)S(1)}, f32[1,32,128]{2,1,0:T(8,128)S(1)}, u32[]{:S(2)}, u32[]{:S(2)}) collective-permute-start(f32[1,32,128]{2,1,0:T(8,128)S(1)} %bitcast.49), channel_id=1, source_target_pairs={{16,0},{32,16},{48,32},{64,48},{80,64},{96,80},{112,96},{17,1},{33... | collective-permute-start | bytes 49160 | tf_op jit(solution)/shard_map/ppermute | solution.py:89
  52.6 4.3 %collective-permute-start.9 = (f32[1,32,128]{2,1,0:T(8,128)S(1)}, f32[1,32,128]{2,1,0:T(8,128)S(1)}, u32[]{:S(2)}, u32[]{:S(2)}) collective-permute-start(f32[1,32,128]{2,1,0:T(8,128)S(1)} %bitcast.48), channel_id=1, source_target_pairs={{0,16},{16,32},{32,48},{48,64},{64,80},{80,96},{96,112},{1,17},{17... | collective-permute-start | bytes 49160 | tf_op jit(solution)/shard_map/ppermute | solution.py:86
  57.0 2.8 %collective-permute-start.2 = (f32[2,66,1,128]{3,2,1,0:T(1,128)S(1)}, f32[2,66,1,128]{3,2,1,0:T(1,128)S(1)}, u32[]{:S(2)}, u32[]{:S(2)}) collective-permute-start(f32[2,66,1,128]{3,2,1,0:T(1,128)S(1)} %get-tuple-element.4), channel_id=1, source_target_pairs={{0,1},{1,2},{2,3},{3,4},{4,5},{5,6},{6,7},{7,8},{8,9},{9,10},{10,1... | collective-permute-start | bytes 202760 | tf_op jit(solution)/shard_map/ppermute | solution.py:86
  59.8 6.1 %collective-permute-start.3 = (f32[2,66,1,128]{3,2,1,0:T(1,128)S(1)}, f32[2,66,1,128]{3,2,1,0:T(1,128)S(1)}, u32[]{:S(2)}, u32[]{:S(2)}) collective-permute-start(f32[2,66,1,128]{3,2,1,0:T(1,128)S(1)} %get-tuple-element.5), channel_id=1, source_target_pairs={{1,0},{2,1},{3,2},{4,3},{5,4},{6,5},{7,6},{8,7},{9,8},{10,9},{11,1... | collective-permute-start | bytes 202760 | tf_op jit(solution)/shard_map/ppermute | solution.py:89
  66.0 2.4 %collective-permute-start.10 = (f32[66,1,128]{2,1,0:T(1,128)S(1)}, f32[66,1,128]{2,1,0:T(1,128)S(1)}, u32[]{:S(2)}, u32[]{:S(2)}) collective-permute-start(f32[66,1,128]{2,1,0:T(1,128)S(1)} %get-tuple-element.18), channel_id=1, source_target_pairs={{1,0},{2,1},{3,2},{4,3},{5,4},{6,5},{7,6},{8,7},{9,8},{10,9},{11,1... | collective-permute-start | bytes 101384 | tf_op jit(solution)/shard_map/ppermute | solution.py:89
  68.4 2.9 %collective-permute-start.11 = (f32[66,1,128]{2,1,0:T(1,128)S(1)}, f32[66,1,128]{2,1,0:T(1,128)S(1)}, u32[]{:S(2)}, u32[]{:S(2)}) collective-permute-start(f32[66,1,128]{2,1,0:T(1,128)S(1)} %get-tuple-element.19), channel_id=1, source_target_pairs={{0,1},{1,2},{2,3},{3,4},{4,5},{5,6},{6,7},{7,8},{8,9},{9,10},{10,1... | collective-permute-start | bytes 101384 | tf_op jit(solution)/shard_map/ppermute | solution.py:86
  72.9 3.8 %collective-permute-done.11 = f32[66,1,128]{2,1,0:T(1,128)S(1)} collective-permute-done((f32[66,1,128]{2,1,0:T(1,128)S(1)}, f32[66,1,128]{2,1,0:T(1,128)S(1)}, u32[]{:S(2)}, u32[]{:S(2)}) %collective-permute-start.11) | collective-permute-done | bytes 33824 | tf_op jit(solution)/shard_map/ppermute | solution.py:86
  78.1 1.9 %collective-permute-start.12 = (f32[1,32,128]{2,1,0:T(8,128)S(1)}, f32[1,32,128]{2,1,0:T(8,128)S(1)}, u32[]{:S(2)}, u32[]{:S(2)}) collective-permute-start(f32[1,32,128]{2,1,0:T(8,128)S(1)} %get-tuple-element.25), channel_id=1, source_target_pairs={{16,0},{32,16},{48,32},{64,48},{80,64},{96,80},{112,96},{17,1},{33... | collective-permute-start | bytes 49160 | tf_op jit(solution)/shard_map/ppermute | solution.py:89
  80.0 4.3 %collective-permute-start.13 = (f32[1,32,128]{2,1,0:T(8,128)S(1)}, f32[1,32,128]{2,1,0:T(8,128)S(1)}, u32[]{:S(2)}, u32[]{:S(2)}) collective-permute-start(f32[1,32,128]{2,1,0:T(8,128)S(1)} %get-tuple-element.24), channel_id=1, source_target_pairs={{0,16},{16,32},{32,48},{48,64},{64,80},{80,96},{96,112},{1,17},{17... | collective-permute-start | bytes 49160 | tf_op jit(solution)/shard_map/ppermute | solution.py:86
  85.4 3.2 %collective-permute-start.14 = (f32[66,1,128]{2,1,0:T(1,128)S(1)}, f32[66,1,128]{2,1,0:T(1,128)S(1)}, u32[]{:S(2)}, u32[]{:S(2)}) collective-permute-start(f32[66,1,128]{2,1,0:T(1,128)S(1)} %get-tuple-element.14), channel_id=1, source_target_pairs={{1,0},{2,1},{3,2},{4,3},{5,4},{6,5},{7,6},{8,7},{9,8},{10,9},{11,1... | collective-permute-start | bytes 101384 | tf_op jit(solution)/shard_map/ppermute | solution.py:89
  88.6 2.1 %collective-permute-start.15 = (f32[66,1,128]{2,1,0:T(1,128)S(1)}, f32[66,1,128]{2,1,0:T(1,128)S(1)}, u32[]{:S(2)}, u32[]{:S(2)}) collective-permute-start(f32[66,1,128]{2,1,0:T(1,128)S(1)} %get-tuple-element.15), channel_id=1, source_target_pairs={{0,1},{1,2},{2,3},{3,4},{4,5},{5,6},{6,7},{7,8},{8,9},{9,10},{10,1... | collective-permute-start | bytes 101384 | tf_op jit(solution)/shard_map/ppermute | solution.py:86
  91.1 5.8 %collective-permute-done.15 = f32[66,1,128]{2,1,0:T(1,128)S(1)} collective-permute-done((f32[66,1,128]{2,1,0:T(1,128)S(1)}, f32[66,1,128]{2,1,0:T(1,128)S(1)}, u32[]{:S(2)}, u32[]{:S(2)}) %collective-permute-start.15) | collective-permute-done | bytes 33824 | tf_op jit(solution)/shard_map/ppermute | solution.py:86
  98.3 1.9 %collective-permute-start.4 = (f32[1,32,128]{2,1,0:T(8,128)S(1)}, f32[1,32,128]{2,1,0:T(8,128)S(1)}, u32[]{:S(2)}, u32[]{:S(2)}) collective-permute-start(f32[1,32,128]{2,1,0:T(8,128)S(1)} %get-tuple-element.29), channel_id=1, source_target_pairs={{16,0},{32,16},{48,32},{64,48},{80,64},{96,80},{112,96},{17,1},{33... | collective-permute-start | bytes 49160 | tf_op jit(solution)/shard_map/ppermute | solution.py:89
  100.3 4.3 %collective-permute-start.5 = (f32[1,32,128]{2,1,0:T(8,128)S(1)}, f32[1,32,128]{2,1,0:T(8,128)S(1)}, u32[]{:S(2)}, u32[]{:S(2)}) collective-permute-start(f32[1,32,128]{2,1,0:T(8,128)S(1)} %get-tuple-element.28), channel_id=1, source_target_pairs={{0,16},{16,32},{32,48},{48,64},{64,80},{80,96},{96,112},{1,17},{17... | collective-permute-start | bytes 49160 | tf_op jit(solution)/shard_map/ppermute | solution.py:86
  105.6 1.9 %collective-permute-start.6 = (f32[66,1,128]{2,1,0:T(1,128)S(1)}, f32[66,1,128]{2,1,0:T(1,128)S(1)}, u32[]{:S(2)}, u32[]{:S(2)}) collective-permute-start(f32[66,1,128]{2,1,0:T(1,128)S(1)} %get-tuple-element.20), channel_id=1, source_target_pairs={{1,0},{2,1},{3,2},{4,3},{5,4},{6,5},{7,6},{8,7},{9,8},{10,9},{11,1... | collective-permute-start | bytes 101384 | tf_op jit(solution)/shard_map/ppermute | solution.py:89
  107.5 3.4 %collective-permute-start.7 = (f32[66,1,128]{2,1,0:T(1,128)S(1)}, f32[66,1,128]{2,1,0:T(1,128)S(1)}, u32[]{:S(2)}, u32[]{:S(2)}) collective-permute-start(f32[66,1,128]{2,1,0:T(1,128)S(1)} %get-tuple-element.21), channel_id=1, source_target_pairs={{0,1},{1,2},{2,3},{3,4},{4,5},{5,6},{6,7},{7,8},{8,9},{9,10},{10,1... | collective-permute-start | bytes 101384 | tf_op jit(solution)/shard_map/ppermute | solution.py:86
  111.3 4.5 %collective-permute-done.7 = f32[66,1,128]{2,1,0:T(1,128)S(1)} collective-permute-done((f32[66,1,128]{2,1,0:T(1,128)S(1)}, f32[66,1,128]{2,1,0:T(1,128)S(1)}, u32[]{:S(2)}, u32[]{:S(2)}) %collective-permute-start.7) | collective-permute-done | bytes 33824 | tf_op jit(solution)/shard_map/ppermute | solution.py:86
  117.2 9.1 %collective-permute-start.16 = (f32[64,32,128]{2,1,0:T(8,128)S(1)}, f32[64,32,128]{2,1,0:T(8,128)S(1)}, u32[]{:S(2)}, u32[]{:S(2)}) collective-permute-start(f32[64,32,128]{2,1,0:T(8,128)S(1)} %fusion.10), channel_id=1, source_target_pairs={{0,128},{128,0},{1,129},{129,1},{2,130},{130,2},{3,131},{131,3},{4... | collective-permute-start | bytes 3145736 | tf_op jit(solution)/shard_map/ppermute | solution.py:164
  126.7 1.7 %fusion.25 = f32[1,64,32,128]{3,2,1,0:T(8,128)} fusion(f32[64,32,128]{2,1,0:T(8,128)S(1)} %fusion.31, f32[64,33,128]{2,1,0:T(8,128)S(1)} %fusion.42, f32[65,32,128]{2,1,0:T(8,128)S(1)} %get-tuple-element.17, f32[1,64,32,128]{3,2,1,0:T(8,128)S(1)} %copy-done.3, f32[64,32,127]{2,1,0:T(8,128)S(1)} %get-tuple-element.23), kind=kLoop, calls=%fused_computation.66 | loop fusion | flops 2359296 | bytes 8380416 | tf_op jit(solution)/shard_map/broadcast_in_dim | solution.py:165
  (49 shorter events, 13.3 us)
Async XLA Ops:
  1.4 55.5 %collective-permute-start = (f32[2,1,32,128]{3,2,1,0:T(8,128)S(1)}, f32[2,1,32,128]{3,2,1,0:T(8,128)S(1)}, u32[]{:S(2)}, u32[]{:S(2)}) collective-permute-start(f32[2,1,32,128]{3,2,1,0:T(8,128)S(1)} %get-tuple-element.6), channel_id=1, source_target_pairs={{0,16},{16,32},{32,48},{48,64},{64,80},{80,96},{96,112},{1,17},{17... | collective-permute-start | bytes 98312 | tf_op jit(solution)/shard_map/ppermute | solution.py:86
  4.9 52.0 %collective-permute-start.1 = (f32[2,1,32,128]{3,2,1,0:T(8,128)S(1)}, f32[2,1,32,128]{3,2,1,0:T(8,128)S(1)}, u32[]{:S(2)}, u32[]{:S(2)}) collective-permute-start(f32[2,1,32,128]{3,2,1,0:T(8,128)S(1)} %get-tuple-element.7), channel_id=1, source_target_pairs={{16,0},{32,16},{48,32},{64,48},{80,64},{96,80},{112,96},{17,1},{33... | collective-permute-start | bytes 98312 | tf_op jit(solution)/shard_map/ppermute | solution.py:89
  47.3 9.6 %copy-start.1 = (f32[1,64,32,128]{3,2,1,0:T(8,128)S(1)}, f32[1,64,32,128]{3,2,1,0:T(8,128)}, u32[]{:S(2)}) copy-start(f32[1,64,32,128]{3,2,1,0:T(8,128)} %param.10) | copy-start | bytes 3145732
  47.3 9.6 %copy-start.2 = (f32[64,32,128]{2,1,0:T(8,128)S(1)}, f32[64,32,128]{2,1,0:T(8,128)}, u32[]{:S(2)}) copy-start(f32[64,32,128]{2,1,0:T(8,128)} %param.7) | copy-start | bytes 3145732
  49.8 16.1 %copy-start = (f32[128,16,128]{2,1,0:T(8,128)S(1)}, f32[128,16,128]{2,1,0:T(8,128)}, u32[]{:S(2)}) copy-start(f32[128,16,128]{2,1,0:T(8,128)} %shard_map.87) | copy-start | bytes 3145732
  50.7 15.2 %collective-permute-start.8 = (f32[1,32,128]{2,1,0:T(8,128)S(1)}, f32[1,32,128]{2,1,0:T(8,128)S(1)}, u32[]{:S(2)}, u32[]{:S(2)}) collective-permute-start(f32[1,32,128]{2,1,0:T(8,128)S(1)} %bitcast.49), channel_id=1, source_target_pairs={{16,0},{32,16},{48,32},{64,48},{80,64},{96,80},{112,96},{17,1},{33... | collective-permute-start | bytes 49160 | tf_op jit(solution)/shard_map/ppermute | solution.py:89
  52.6 13.3 %collective-permute-start.9 = (f32[1,32,128]{2,1,0:T(8,128)S(1)}, f32[1,32,128]{2,1,0:T(8,128)S(1)}, u32[]{:S(2)}, u32[]{:S(2)}) collective-permute-start(f32[1,32,128]{2,1,0:T(8,128)S(1)} %bitcast.48), channel_id=1, source_target_pairs={{0,16},{16,32},{32,48},{48,64},{64,80},{80,96},{96,112},{1,17},{17... | collective-permute-start | bytes 49160 | tf_op jit(solution)/shard_map/ppermute | solution.py:86
  57.0 14.3 %collective-permute-start.2 = (f32[2,66,1,128]{3,2,1,0:T(1,128)S(1)}, f32[2,66,1,128]{3,2,1,0:T(1,128)S(1)}, u32[]{:S(2)}, u32[]{:S(2)}) collective-permute-start(f32[2,66,1,128]{3,2,1,0:T(1,128)S(1)} %get-tuple-element.4), channel_id=1, source_target_pairs={{0,1},{1,2},{2,3},{3,4},{4,5},{5,6},{6,7},{7,8},{8,9},{9,10},{10,1... | collective-permute-start | bytes 202760 | tf_op jit(solution)/shard_map/ppermute | solution.py:86
  59.8 11.5 %collective-permute-start.3 = (f32[2,66,1,128]{3,2,1,0:T(1,128)S(1)}, f32[2,66,1,128]{3,2,1,0:T(1,128)S(1)}, u32[]{:S(2)}, u32[]{:S(2)}) collective-permute-start(f32[2,66,1,128]{3,2,1,0:T(1,128)S(1)} %get-tuple-element.5), channel_id=1, source_target_pairs={{1,0},{2,1},{3,2},{4,3},{5,4},{6,5},{7,6},{8,7},{9,8},{10,9},{11,1... | collective-permute-start | bytes 202760 | tf_op jit(solution)/shard_map/ppermute | solution.py:89
  66.0 6.9 %collective-permute-start.10 = (f32[66,1,128]{2,1,0:T(1,128)S(1)}, f32[66,1,128]{2,1,0:T(1,128)S(1)}, u32[]{:S(2)}, u32[]{:S(2)}) collective-permute-start(f32[66,1,128]{2,1,0:T(1,128)S(1)} %get-tuple-element.18), channel_id=1, source_target_pairs={{1,0},{2,1},{3,2},{4,3},{5,4},{6,5},{7,6},{8,7},{9,8},{10,9},{11,1... | collective-permute-start | bytes 101384 | tf_op jit(solution)/shard_map/ppermute | solution.py:89
  68.4 8.3 %collective-permute-start.11 = (f32[66,1,128]{2,1,0:T(1,128)S(1)}, f32[66,1,128]{2,1,0:T(1,128)S(1)}, u32[]{:S(2)}, u32[]{:S(2)}) collective-permute-start(f32[66,1,128]{2,1,0:T(1,128)S(1)} %get-tuple-element.19), channel_id=1, source_target_pairs={{0,1},{1,2},{2,3},{3,4},{4,5},{5,6},{6,7},{7,8},{8,9},{9,10},{10,1... | collective-permute-start | bytes 101384 | tf_op jit(solution)/shard_map/ppermute | solution.py:86
  72.9 4.3 %copy-start.3 = (f32[1,64,32,128]{3,2,1,0:T(8,128)S(1)}, f32[1,64,32,128]{3,2,1,0:T(8,128)}, u32[]{:S(2)}) copy-start(f32[1,64,32,128]{3,2,1,0:T(8,128)} %param.8) | copy-start | bytes 3145732
  72.9 4.3 %copy-start.4 = (f32[1,64,32,128]{3,2,1,0:T(8,128)S(1)}, f32[1,64,32,128]{3,2,1,0:T(8,128)}, u32[]{:S(2)}) copy-start(f32[1,64,32,128]{3,2,1,0:T(8,128)} %param.9) | copy-start | bytes 3145732
  78.1 7.2 %collective-permute-start.12 = (f32[1,32,128]{2,1,0:T(8,128)S(1)}, f32[1,32,128]{2,1,0:T(8,128)S(1)}, u32[]{:S(2)}, u32[]{:S(2)}) collective-permute-start(f32[1,32,128]{2,1,0:T(8,128)S(1)} %get-tuple-element.25), channel_id=1, source_target_pairs={{16,0},{32,16},{48,32},{64,48},{80,64},{96,80},{112,96},{17,1},{33... | collective-permute-start | bytes 49160 | tf_op jit(solution)/shard_map/ppermute | solution.py:89
  80.0 5.3 %collective-permute-start.13 = (f32[1,32,128]{2,1,0:T(8,128)S(1)}, f32[1,32,128]{2,1,0:T(8,128)S(1)}, u32[]{:S(2)}, u32[]{:S(2)}) collective-permute-start(f32[1,32,128]{2,1,0:T(8,128)S(1)} %get-tuple-element.24), channel_id=1, source_target_pairs={{0,16},{16,32},{32,48},{48,64},{64,80},{80,96},{96,112},{1,17},{17... | collective-permute-start | bytes 49160 | tf_op jit(solution)/shard_map/ppermute | solution.py:86
  85.4 5.7 %collective-permute-start.14 = (f32[66,1,128]{2,1,0:T(1,128)S(1)}, f32[66,1,128]{2,1,0:T(1,128)S(1)}, u32[]{:S(2)}, u32[]{:S(2)}) collective-permute-start(f32[66,1,128]{2,1,0:T(1,128)S(1)} %get-tuple-element.14), channel_id=1, source_target_pairs={{1,0},{2,1},{3,2},{4,3},{5,4},{6,5},{7,6},{8,7},{9,8},{10,9},{11,1... | collective-permute-start | bytes 101384 | tf_op jit(solution)/shard_map/ppermute | solution.py:89
  88.6 8.3 %collective-permute-start.15 = (f32[66,1,128]{2,1,0:T(1,128)S(1)}, f32[66,1,128]{2,1,0:T(1,128)S(1)}, u32[]{:S(2)}, u32[]{:S(2)}) collective-permute-start(f32[66,1,128]{2,1,0:T(1,128)S(1)} %get-tuple-element.15), channel_id=1, source_target_pairs={{0,1},{1,2},{2,3},{3,4},{4,5},{5,6},{6,7},{7,8},{8,9},{9,10},{10,1... | collective-permute-start | bytes 101384 | tf_op jit(solution)/shard_map/ppermute | solution.py:86
  98.3 7.2 %collective-permute-start.4 = (f32[1,32,128]{2,1,0:T(8,128)S(1)}, f32[1,32,128]{2,1,0:T(8,128)S(1)}, u32[]{:S(2)}, u32[]{:S(2)}) collective-permute-start(f32[1,32,128]{2,1,0:T(8,128)S(1)} %get-tuple-element.29), channel_id=1, source_target_pairs={{16,0},{32,16},{48,32},{64,48},{80,64},{96,80},{112,96},{17,1},{33... | collective-permute-start | bytes 49160 | tf_op jit(solution)/shard_map/ppermute | solution.py:89
  100.3 5.2 %collective-permute-start.5 = (f32[1,32,128]{2,1,0:T(8,128)S(1)}, f32[1,32,128]{2,1,0:T(8,128)S(1)}, u32[]{:S(2)}, u32[]{:S(2)}) collective-permute-start(f32[1,32,128]{2,1,0:T(8,128)S(1)} %get-tuple-element.28), channel_id=1, source_target_pairs={{0,16},{16,32},{32,48},{48,64},{64,80},{80,96},{96,112},{1,17},{17... | collective-permute-start | bytes 49160 | tf_op jit(solution)/shard_map/ppermute | solution.py:86
  105.6 5.7 %collective-permute-start.6 = (f32[66,1,128]{2,1,0:T(1,128)S(1)}, f32[66,1,128]{2,1,0:T(1,128)S(1)}, u32[]{:S(2)}, u32[]{:S(2)}) collective-permute-start(f32[66,1,128]{2,1,0:T(1,128)S(1)} %get-tuple-element.20), channel_id=1, source_target_pairs={{1,0},{2,1},{3,2},{4,3},{5,4},{6,5},{7,6},{8,7},{9,8},{10,9},{11,1... | collective-permute-start | bytes 101384 | tf_op jit(solution)/shard_map/ppermute | solution.py:89
  107.5 8.3 %collective-permute-start.7 = (f32[66,1,128]{2,1,0:T(1,128)S(1)}, f32[66,1,128]{2,1,0:T(1,128)S(1)}, u32[]{:S(2)}, u32[]{:S(2)}) collective-permute-start(f32[66,1,128]{2,1,0:T(1,128)S(1)} %get-tuple-element.21), channel_id=1, source_target_pairs={{0,1},{1,2},{2,3},{3,4},{4,5},{5,6},{6,7},{7,8},{8,9},{9,10},{10,1... | collective-permute-start | bytes 101384 | tf_op jit(solution)/shard_map/ppermute | solution.py:86
  117.2 11.4 %collective-permute-start.16 = (f32[64,32,128]{2,1,0:T(8,128)S(1)}, f32[64,32,128]{2,1,0:T(8,128)S(1)}, u32[]{:S(2)}, u32[]{:S(2)}) collective-permute-start(f32[64,32,128]{2,1,0:T(8,128)S(1)} %fusion.10), channel_id=1, source_target_pairs={{0,128},{128,0},{1,129},{129,1},{2,130},{130,2},{3,131},{131,3},{4... | collective-permute-start | bytes 3145736 | tf_op jit(solution)/shard_map/ppermute | solution.py:164

commit v2 on v1

--- a/solution.py
+++ b/solution.py
@@ -11,14 +11,20 @@
 step_size = 0.12
 
 
-def exchange_kernel(n_ty, tiles, src, dst, send_sem, recv_sem, local_sem):
+def exchange_kernel(n_ty, tiles, rows, step, store, dst, saved, src, send_sem, recv_sem, local_sem, load_sem):
     scen = lax.axis_index("scen")
     me = lax.axis_index("tx") * n_ty + lax.axis_index("ty")
+    lanes = src.shape[1]
+    load = pltpu.make_async_copy(store, saved, load_sem)
+    load.start()
 
     def device(k):
         t = (me + k) % tiles
         return t, (scen, t // n_ty, t % n_ty)
 
+    def piece(t):
+        return pl.ds(pl.multiple_of(t * rows, rows), rows)
+
     barrier = pltpu.get_barrier_semaphore()
 
     def greet(k, carry):
@@ -26,15 +32,26 @@
         return carry
 
     lax.fori_loop(1, tiles, greet, 0)
+    load.wait()
+    chosen = step[0]
+
+    def unfold(g, carry):
+        for r in range(rows):
+            src[pl.ds(g * 8 * rows + r, 8, stride=rows), :] = saved[
+                chosen, pl.ds(pl.multiple_of(g * 8, 8), 8), pl.ds(r * lanes, lanes)
+            ]
+        return carry
+
+    lax.fori_loop(0, tiles // 8, unfold, 0)
     pl.semaphore_wait(barrier, tiles - 1)
-    own = pltpu.make_async_copy(src.at[me], dst.at[me], local_sem)
+    own = pltpu.make_async_copy(src.at[piece(me)], dst.at[piece(me)], local_sem)
     own.start()
 
     def send(k, carry):
         t, target = device(k)
         pltpu.make_async_remote_copy(
-            src_ref=src.at[t],
-            dst_ref=dst.at[me],
+            src_ref=src.at[piece(t)],
+            dst_ref=dst.at[piece(me)],
             send_sem=send_sem,
             recv_sem=recv_sem,
             device_id=target,
@@ -44,21 +61,33 @@
 
     lax.fori_loop(1, tiles, send, 0)
     own.wait()
-    others = pl.ds(0, tiles - 1)
+    others = pl.ds(0, (tiles - 1) * rows)
     pltpu.make_async_copy(src.at[others], src.at[others], send_sem).wait()
     pltpu.make_async_copy(dst.at[others], dst.at[others], recv_sem).wait()
 
 
-def exchange(pieces, n_ty):
-    tiles = pieces.shape[0]
-    return pl.pallas_call(
-        functools.partial(exchange_kernel, n_ty, tiles),
-        out_shape=jax.ShapeDtypeStruct(pieces.shape, pieces.dtype),
-        in_specs=[pl.BlockSpec(memory_space=pltpu.VMEM)],
+def exchange(store, step_index, n_ty, lanes):
+    tiles, piece = store.shape[1:]
+    rows = piece // lanes
+    flat = (tiles * rows, lanes)
+    arrived = pl.pallas_call(
+        functools.partial(exchange_kernel, n_ty, tiles, rows),
+        out_shape=jax.ShapeDtypeStruct(flat, store.dtype),
+        in_specs=[
+            pl.BlockSpec(memory_space=pltpu.SMEM),
+            pl.BlockSpec(memory_space=pltpu.HBM),
+        ],
         out_specs=pl.BlockSpec(memory_space=pltpu.VMEM),
-        scratch_shapes=[pltpu.SemaphoreType.DMA] * 3,
-        compiler_params=pltpu.CompilerParams(collective_id=0, has_side_effects=True),
-    )(pieces)
+        scratch_shapes=[
+            pltpu.VMEM(store.shape, store.dtype),
+            pltpu.VMEM(flat, store.dtype),
+            *[pltpu.SemaphoreType.DMA] * 4,
+        ],
+        compiler_params=pltpu.CompilerParams(
+            collective_id=0, has_side_effects=True, vmem_limit_bytes=32 << 20
+        ),
+    )(step_index, store)
+    return arrived.reshape(tiles, rows, lanes)
 
 
 def assemble_kernel(holder, arrived, state):
@@ -138,8 +167,7 @@
 
 def local(conductivity, cooling, source, adjoint_in, store, holder, step_index):
     cells_x, cells_y, cells_z = conductivity.shape
-    chosen = lax.dynamic_index_in_dim(store[0, :, 0], step_index[0], 0, keepdims=False)
-    arrived = exchange(chosen.reshape(chosen.shape[0], -1, cells_z), lax.axis_size("ty"))
+    arrived = exchange(store[0, :, 0], step_index, lax.axis_size("ty"), cells_z)
     state_zero = assemble(arrived, holder[0]).reshape(cells_x, cells_y, cells_z)
     cool_here = cooling[0]
     heat_here = source[0]

time: 132 us -> 132 us (level)
  Pallas kernels: 39.9 us -> 38.5 us
    pallas_call x1, Pallas kernels: 37.3 us -> 36 us  [exchange(): pl.pallas_call(functools.partial(exchange_kernel, n_ty, tiles, rows), out...]
    unnamed x12 -> x14, local copies, waits for them, and re-layouts: 2.51 us -> 3.77 us
  transfers between devices with their start and end apart: 17 -> 17, of which waited for: 4 -> 3; matrix products, arithmetic and copies ran while one was open for 8% -> 6% of each run, Pallas kernels for 31% -> 30%
where the time goes in v2:
time: 132 us; the launch traced here: 130 us
  starting transfers between devices  57.8 us (44%)
  Pallas kernels  38.5 us (29%)
  waiting for transfers between devices  14.1 us (11%)
  other arithmetic  12.7 us (10%)
  local copies, waits for them, and re-layouts  4.78 us (4%)
  between operations  1.7 us (1%)
    pallas_call x1, Pallas kernels, exchange(): pl.pallas_call(functools.partial(exchange_kernel, n_ty, tiles, rows), out...  36 us
    ppermute x8, starting transfers between devices, padded_2(): lax.ppermute(lax.slice_in_dim(block, block.shape[dim] - width, None, axis...  27.4 us
    ppermute x8, starting transfers between devices, padded_2(): lax.ppermute(lax.slice_in_dim(block, 0, width, axis=dim), axis, backward)  21.3 us
    ppermute x8, waiting for transfers between devices, padded_2(): lax.ppermute(lax.slice_in_dim(block, block.shape[dim] - width, None, axis...  14 us
    ppermute x1, starting transfers between devices, local(): summed = gradient + lax.ppermute(gradient, 'scen', [(0, 1), (1, 0)])  9.14 us
    unnamed x14, local copies, waits for them, and re-layouts  3.77 us
  transfers between devices with their start and end apart: 17, of which 3 were waited for; matrix products, arithmetic and copies ran while one was open for 6% of the time, Pallas kernels for 30%

profile of v2, /device:TPU:7, one launch (start us, length us, event | category | flops | bytes accessed | tf_op | source)
XLA Modules:
  0.0 129.6 jit_solution(432658082315861413)
XLA Ops:
  1.4 3.5 %collective-permute-start = (f32[2,1,32,128]{3,2,1,0:T(8,128)S(1)}, f32[2,1,32,128]{3,2,1,0:T(8,128)S(1)}, u32[]{:S(2)}, u32[]{:S(2)}) collective-permute-start(f32[2,1,32,128]{3,2,1,0:T(8,128)S(1)} %get-tuple-element.6), channel_id=1, source_target_pairs={{0,16},{16,32},{32,48},{48,64},{64,80},{80,96},{96,112},{1,17},{17... | collective-permute-start | bytes 98312 | tf_op jit(solution)/shard_map/ppermute | solution.py:115
  4.9 1.9 %collective-permute-start.1 = (f32[2,1,32,128]{3,2,1,0:T(8,128)S(1)}, f32[2,1,32,128]{3,2,1,0:T(8,128)S(1)}, u32[]{:S(2)}, u32[]{:S(2)}) collective-permute-start(f32[2,1,32,128]{3,2,1,0:T(8,128)S(1)} %get-tuple-element.7), channel_id=1, source_target_pairs={{16,0},{32,16},{48,32},{64,48},{80,64},{96,80},{112,96},{17,1},{33... | collective-permute-start | bytes 98312 | tf_op jit(solution)/shard_map/ppermute | solution.py:118
  7.5 2.8 %copy-done = f32[1,6,1,128,2048]{4,3,2,1,0:T(8,128)S(1)} copy-done((f32[1,6,1,128,2048]{4,3,2,1,0:T(8,128)S(1)}, f32[1,6,1,128,2048]{4,3,2,1,0:T(8,128)}, u32[]{:S(2)}) %copy-start) | copy-done | bytes 6291480
  10.2 36.0 %shard_map.86 = f32[2048,128]{1,0:T(8,128)S(1)} custom-call(s32[1]{0:T(128)S(6)} %copy.9.step, f32[6,128,2048]{2,1,0:T(8,128)S(1)} %bitcast.29), custom_call_target="tpu_custom_call" | custom-call | tf_op jit(solution)/shard_map/pallas_call | solution.py:73
  47.2 2.6 %shard_map.87 = f32[128,16,128]{2,1,0:T(8,128)} custom-call(s32[128]{0:T(128)} %bitcast.44, f32[128,16,128]{2,1,0:T(8,128)} %bitcast.30), custom_call_target="tpu_custom_call" | custom-call | tf_op jit(solution)/shard_map/pallas_call | solution.py:102
  50.6 1.9 %collective-permute-start.8 = (f32[1,32,128]{2,1,0:T(8,128)S(1)}, f32[1,32,128]{2,1,0:T(8,128)S(1)}, u32[]{:S(2)}, u32[]{:S(2)}) collective-permute-start(f32[1,32,128]{2,1,0:T(8,128)S(1)} %bitcast.43), channel_id=1, source_target_pairs={{16,0},{32,16},{48,32},{64,48},{80,64},{96,80},{112,96},{17,1},{33... | collective-permute-start | bytes 49160 | tf_op jit(solution)/shard_map/ppermute | solution.py:118
  52.5 4.3 %collective-permute-start.9 = (f32[1,32,128]{2,1,0:T(8,128)S(1)}, f32[1,32,128]{2,1,0:T(8,128)S(1)}, u32[]{:S(2)}, u32[]{:S(2)}) collective-permute-start(f32[1,32,128]{2,1,0:T(8,128)S(1)} %bitcast.42), channel_id=1, source_target_pairs={{0,16},{16,32},{32,48},{48,64},{64,80},{80,96},{96,112},{1,17},{17... | collective-permute-start | bytes 49160 | tf_op jit(solution)/shard_map/ppermute | solution.py:115
  56.9 2.8 %collective-permute-start.2 = (f32[2,66,1,128]{3,2,1,0:T(1,128)S(1)}, f32[2,66,1,128]{3,2,1,0:T(1,128)S(1)}, u32[]{:S(2)}, u32[]{:S(2)}) collective-permute-start(f32[2,66,1,128]{3,2,1,0:T(1,128)S(1)} %get-tuple-element.4), channel_id=1, source_target_pairs={{0,1},{1,2},{2,3},{3,4},{4,5},{5,6},{6,7},{7,8},{8,9},{9,10},{10,1... | collective-permute-start | bytes 202760 | tf_op jit(solution)/shard_map/ppermute | solution.py:115
  59.7 6.1 %collective-permute-start.3 = (f32[2,66,1,128]{3,2,1,0:T(1,128)S(1)}, f32[2,66,1,128]{3,2,1,0:T(1,128)S(1)}, u32[]{:S(2)}, u32[]{:S(2)}) collective-permute-start(f32[2,66,1,128]{3,2,1,0:T(1,128)S(1)} %get-tuple-element.5), channel_id=1, source_target_pairs={{1,0},{2,1},{3,2},{4,3},{5,4},{6,5},{7,6},{8,7},{9,8},{10,9},{11,1... | collective-permute-start | bytes 202760 | tf_op jit(solution)/shard_map/ppermute | solution.py:118
  65.9 2.4 %collective-permute-start.10 = (f32[66,1,128]{2,1,0:T(1,128)S(1)}, f32[66,1,128]{2,1,0:T(1,128)S(1)}, u32[]{:S(2)}, u32[]{:S(2)}) collective-permute-start(f32[66,1,128]{2,1,0:T(1,128)S(1)} %get-tuple-element.18), channel_id=1, source_target_pairs={{1,0},{2,1},{3,2},{4,3},{5,4},{6,5},{7,6},{8,7},{9,8},{10,9},{11,1... | collective-permute-start | bytes 101384 | tf_op jit(solution)/shard_map/ppermute | solution.py:118
  68.3 2.9 %collective-permute-start.11 = (f32[66,1,128]{2,1,0:T(1,128)S(1)}, f32[66,1,128]{2,1,0:T(1,128)S(1)}, u32[]{:S(2)}, u32[]{:S(2)}) collective-permute-start(f32[66,1,128]{2,1,0:T(1,128)S(1)} %get-tuple-element.19), channel_id=1, source_target_pairs={{0,1},{1,2},{2,3},{3,4},{4,5},{5,6},{6,7},{7,8},{8,9},{9,10},{10,1... | collective-permute-start | bytes 101384 | tf_op jit(solution)/shard_map/ppermute | solution.py:115
  72.8 3.8 %collective-permute-done.11 = f32[66,1,128]{2,1,0:T(1,128)S(1)} collective-permute-done((f32[66,1,128]{2,1,0:T(1,128)S(1)}, f32[66,1,128]{2,1,0:T(1,128)S(1)}, u32[]{:S(2)}, u32[]{:S(2)}) %collective-permute-start.11) | collective-permute-done | bytes 33824 | tf_op jit(solution)/shard_map/ppermute | solution.py:115
  77.9 1.9 %collective-permute-start.12 = (f32[1,32,128]{2,1,0:T(8,128)S(1)}, f32[1,32,128]{2,1,0:T(8,128)S(1)}, u32[]{:S(2)}, u32[]{:S(2)}) collective-permute-start(f32[1,32,128]{2,1,0:T(8,128)S(1)} %get-tuple-element.25), channel_id=1, source_target_pairs={{16,0},{32,16},{48,32},{64,48},{80,64},{96,80},{112,96},{17,1},{33... | collective-permute-start | bytes 49160 | tf_op jit(solution)/shard_map/ppermute | solution.py:118
  79.9 4.3 %collective-permute-start.13 = (f32[1,32,128]{2,1,0:T(8,128)S(1)}, f32[1,32,128]{2,1,0:T(8,128)S(1)}, u32[]{:S(2)}, u32[]{:S(2)}) collective-permute-start(f32[1,32,128]{2,1,0:T(8,128)S(1)} %get-tuple-element.24), channel_id=1, source_target_pairs={{0,16},{16,32},{32,48},{48,64},{64,80},{80,96},{96,112},{1,17},{17... | collective-permute-start | bytes 49160 | tf_op jit(solution)/shard_map/ppermute | solution.py:115
  85.2 3.2 %collective-permute-start.14 = (f32[66,1,128]{2,1,0:T(1,128)S(1)}, f32[66,1,128]{2,1,0:T(1,128)S(1)}, u32[]{:S(2)}, u32[]{:S(2)}) collective-permute-start(f32[66,1,128]{2,1,0:T(1,128)S(1)} %get-tuple-element.14), channel_id=1, source_target_pairs={{1,0},{2,1},{3,2},{4,3},{5,4},{6,5},{7,6},{8,7},{9,8},{10,9},{11,1... | collective-permute-start | bytes 101384 | tf_op jit(solution)/shard_map/ppermute | solution.py:118
  88.4 2.1 %collective-permute-start.15 = (f32[66,1,128]{2,1,0:T(1,128)S(1)}, f32[66,1,128]{2,1,0:T(1,128)S(1)}, u32[]{:S(2)}, u32[]{:S(2)}) collective-permute-start(f32[66,1,128]{2,1,0:T(1,128)S(1)} %get-tuple-element.15), channel_id=1, source_target_pairs={{0,1},{1,2},{2,3},{3,4},{4,5},{5,6},{6,7},{7,8},{8,9},{9,10},{10,1... | collective-permute-start | bytes 101384 | tf_op jit(solution)/shard_map/ppermute | solution.py:115
  90.9 5.8 %collective-permute-done.15 = f32[66,1,128]{2,1,0:T(1,128)S(1)} collective-permute-done((f32[66,1,128]{2,1,0:T(1,128)S(1)}, f32[66,1,128]{2,1,0:T(1,128)S(1)}, u32[]{:S(2)}, u32[]{:S(2)}) %collective-permute-start.15) | collective-permute-done | bytes 33824 | tf_op jit(solution)/shard_map/ppermute | solution.py:115
  98.2 1.9 %collective-permute-start.4 = (f32[1,32,128]{2,1,0:T(8,128)S(1)}, f32[1,32,128]{2,1,0:T(8,128)S(1)}, u32[]{:S(2)}, u32[]{:S(2)}) collective-permute-start(f32[1,32,128]{2,1,0:T(8,128)S(1)} %get-tuple-element.29), channel_id=1, source_target_pairs={{16,0},{32,16},{48,32},{64,48},{80,64},{96,80},{112,96},{17,1},{33... | collective-permute-start | bytes 49160 | tf_op jit(solution)/shard_map/ppermute | solution.py:118
  100.1 4.3 %collective-permute-start.5 = (f32[1,32,128]{2,1,0:T(8,128)S(1)}, f32[1,32,128]{2,1,0:T(8,128)S(1)}, u32[]{:S(2)}, u32[]{:S(2)}) collective-permute-start(f32[1,32,128]{2,1,0:T(8,128)S(1)} %get-tuple-element.28), channel_id=1, source_target_pairs={{0,16},{16,32},{32,48},{48,64},{64,80},{80,96},{96,112},{1,17},{17... | collective-permute-start | bytes 49160 | tf_op jit(solution)/shard_map/ppermute | solution.py:115
  105.4 1.9 %collective-permute-start.6 = (f32[66,1,128]{2,1,0:T(1,128)S(1)}, f32[66,1,128]{2,1,0:T(1,128)S(1)}, u32[]{:S(2)}, u32[]{:S(2)}) collective-permute-start(f32[66,1,128]{2,1,0:T(1,128)S(1)} %get-tuple-element.20), channel_id=1, source_target_pairs={{1,0},{2,1},{3,2},{4,3},{5,4},{6,5},{7,6},{8,7},{9,8},{10,9},{11,1... | collective-permute-start | bytes 101384 | tf_op jit(solution)/shard_map/ppermute | solution.py:118
  107.4 3.4 %collective-permute-start.7 = (f32[66,1,128]{2,1,0:T(1,128)S(1)}, f32[66,1,128]{2,1,0:T(1,128)S(1)}, u32[]{:S(2)}, u32[]{:S(2)}) collective-permute-start(f32[66,1,128]{2,1,0:T(1,128)S(1)} %get-tuple-element.21), channel_id=1, source_target_pairs={{0,1},{1,2},{2,3},{3,4},{4,5},{5,6},{6,7},{7,8},{8,9},{9,10},{10,1... | collective-permute-start | bytes 101384 | tf_op jit(solution)/shard_map/ppermute | solution.py:115
  111.2 4.5 %collective-permute-done.7 = f32[66,1,128]{2,1,0:T(1,128)S(1)} collective-permute-done((f32[66,1,128]{2,1,0:T(1,128)S(1)}, f32[66,1,128]{2,1,0:T(1,128)S(1)}, u32[]{:S(2)}, u32[]{:S(2)}) %collective-permute-start.7) | collective-permute-done | bytes 33824 | tf_op jit(solution)/shard_map/ppermute | solution.py:115
  117.0 9.1 %collective-permute-start.16 = (f32[64,32,128]{2,1,0:T(8,128)S(1)}, f32[64,32,128]{2,1,0:T(8,128)S(1)}, u32[]{:S(2)}, u32[]{:S(2)}) collective-permute-start(f32[64,32,128]{2,1,0:T(8,128)S(1)} %fusion.10), channel_id=1, source_target_pairs={{0,128},{128,0},{1,129},{129,1},{2,130},{130,2},{3,131},{131,3},{4... | collective-permute-start | bytes 3145736 | tf_op jit(solution)/shard_map/ppermute | solution.py:192
  126.6 1.8 %fusion.25 = f32[1,64,32,128]{3,2,1,0:T(8,128)} fusion(f32[64,32,128]{2,1,0:T(8,128)S(1)} %fusion.31, f32[64,33,128]{2,1,0:T(8,128)S(1)} %fusion.42, f32[65,32,128]{2,1,0:T(8,128)S(1)} %get-tuple-element.17, f32[1,64,32,128]{3,2,1,0:T(8,128)S(1)} %copy-done.5, f32[64,32,127]{2,1,0:T(8,128)S(1)} %get-tuple-element.23), kind=kLoop, calls=%fused_computation.66 | loop fusion | flops 2359296 | bytes 8380416 | tf_op jit(solution)/shard_map/broadcast_in_dim | solution.py:193
  (51 shorter events, 13.0 us)
Async XLA Ops:
  1.4 55.4 %collective-permute-start = (f32[2,1,32,128]{3,2,1,0:T(8,128)S(1)}, f32[2,1,32,128]{3,2,1,0:T(8,128)S(1)}, u32[]{:S(2)}, u32[]{:S(2)}) collective-permute-start(f32[2,1,32,128]{3,2,1,0:T(8,128)S(1)} %get-tuple-element.6), channel_id=1, source_target_pairs={{0,16},{16,32},{32,48},{48,64},{64,80},{80,96},{96,112},{1,17},{17... | collective-permute-start | bytes 98312 | tf_op jit(solution)/shard_map/ppermute | solution.py:115
  4.9 51.9 %collective-permute-start.1 = (f32[2,1,32,128]{3,2,1,0:T(8,128)S(1)}, f32[2,1,32,128]{3,2,1,0:T(8,128)S(1)}, u32[]{:S(2)}, u32[]{:S(2)}) collective-permute-start(f32[2,1,32,128]{3,2,1,0:T(8,128)S(1)} %get-tuple-element.7), channel_id=1, source_target_pairs={{16,0},{32,16},{48,32},{64,48},{80,64},{96,80},{112,96},{17,1},{33... | collective-permute-start | bytes 98312 | tf_op jit(solution)/shard_map/ppermute | solution.py:118
  7.4 2.8 %copy-start = (f32[1,6,1,128,2048]{4,3,2,1,0:T(8,128)S(1)}, f32[1,6,1,128,2048]{4,3,2,1,0:T(8,128)}, u32[]{:S(2)}) copy-start(f32[1,6,1,128,2048]{4,3,2,1,0:T(8,128)} %param.11) | copy-start | bytes 18874372
  46.2 1.0 copy-start.1
  47.2 9.6 %copy-start.3 = (f32[1,64,32,128]{3,2,1,0:T(8,128)S(1)}, f32[1,64,32,128]{3,2,1,0:T(8,128)}, u32[]{:S(2)}) copy-start(f32[1,64,32,128]{3,2,1,0:T(8,128)} %param.10) | copy-start | bytes 3145732
  47.2 9.6 %copy-start.4 = (f32[64,32,128]{2,1,0:T(8,128)S(1)}, f32[64,32,128]{2,1,0:T(8,128)}, u32[]{:S(2)}) copy-start(f32[64,32,128]{2,1,0:T(8,128)} %param.7) | copy-start | bytes 3145732
  49.7 16.1 %copy-start.2 = (f32[128,16,128]{2,1,0:T(8,128)S(1)}, f32[128,16,128]{2,1,0:T(8,128)}, u32[]{:S(2)}) copy-start(f32[128,16,128]{2,1,0:T(8,128)} %shard_map.87) | copy-start | bytes 3145732
  50.6 15.2 %collective-permute-start.8 = (f32[1,32,128]{2,1,0:T(8,128)S(1)}, f32[1,32,128]{2,1,0:T(8,128)S(1)}, u32[]{:S(2)}, u32[]{:S(2)}) collective-permute-start(f32[1,32,128]{2,1,0:T(8,128)S(1)} %bitcast.43), channel_id=1, source_target_pairs={{16,0},{32,16},{48,32},{64,48},{80,64},{96,80},{112,96},{17,1},{33... | collective-permute-start | bytes 49160 | tf_op jit(solution)/shard_map/ppermute | solution.py:118
  52.5 13.3 %collective-permute-start.9 = (f32[1,32,128]{2,1,0:T(8,128)S(1)}, f32[1,32,128]{2,1,0:T(8,128)S(1)}, u32[]{:S(2)}, u32[]{:S(2)}) collective-permute-start(f32[1,32,128]{2,1,0:T(8,128)S(1)} %bitcast.42), channel_id=1, source_target_pairs={{0,16},{16,32},{32,48},{48,64},{64,80},{80,96},{96,112},{1,17},{17... | collective-permute-start | bytes 49160 | tf_op jit(solution)/shard_map/ppermute | solution.py:115
  56.9 14.3 %collective-permute-start.2 = (f32[2,66,1,128]{3,2,1,0:T(1,128)S(1)}, f32[2,66,1,128]{3,2,1,0:T(1,128)S(1)}, u32[]{:S(2)}, u32[]{:S(2)}) collective-permute-start(f32[2,66,1,128]{3,2,1,0:T(1,128)S(1)} %get-tuple-element.4), channel_id=1, source_target_pairs={{0,1},{1,2},{2,3},{3,4},{4,5},{5,6},{6,7},{7,8},{8,9},{9,10},{10,1... | collective-permute-start | bytes 202760 | tf_op jit(solution)/shard_map/ppermute | solution.py:115
  59.7 11.5 %collective-permute-start.3 = (f32[2,66,1,128]{3,2,1,0:T(1,128)S(1)}, f32[2,66,1,128]{3,2,1,0:T(1,128)S(1)}, u32[]{:S(2)}, u32[]{:S(2)}) collective-permute-start(f32[2,66,1,128]{3,2,1,0:T(1,128)S(1)} %get-tuple-element.5), channel_id=1, source_target_pairs={{1,0},{2,1},{3,2},{4,3},{5,4},{6,5},{7,6},{8,7},{9,8},{10,9},{11,1... | collective-permute-start | bytes 202760 | tf_op jit(solution)/shard_map/ppermute | solution.py:118
  65.9 6.9 %collective-permute-start.10 = (f32[66,1,128]{2,1,0:T(1,128)S(1)}, f32[66,1,128]{2,1,0:T(1,128)S(1)}, u32[]{:S(2)}, u32[]{:S(2)}) collective-permute-start(f32[66,1,128]{2,1,0:T(1,128)S(1)} %get-tuple-element.18), channel_id=1, source_target_pairs={{1,0},{2,1},{3,2},{4,3},{5,4},{6,5},{7,6},{8,7},{9,8},{10,9},{11,1... | collective-permute-start | bytes 101384 | tf_op jit(solution)/shard_map/ppermute | solution.py:118
  68.3 8.3 %collective-permute-start.11 = (f32[66,1,128]{2,1,0:T(1,128)S(1)}, f32[66,1,128]{2,1,0:T(1,128)S(1)}, u32[]{:S(2)}, u32[]{:S(2)}) collective-permute-start(f32[66,1,128]{2,1,0:T(1,128)S(1)} %get-tuple-element.19), channel_id=1, source_target_pairs={{0,1},{1,2},{2,3},{3,4},{4,5},{5,6},{6,7},{7,8},{8,9},{9,10},{10,1... | collective-permute-start | bytes 101384 | tf_op jit(solution)/shard_map/ppermute | solution.py:115
  72.8 4.3 %copy-start.5 = (f32[1,64,32,128]{3,2,1,0:T(8,128)S(1)}, f32[1,64,32,128]{3,2,1,0:T(8,128)}, u32[]{:S(2)}) copy-start(f32[1,64,32,128]{3,2,1,0:T(8,128)} %param.8) | copy-start | bytes 3145732
  72.8 4.3 %copy-start.6 = (f32[1,64,32,128]{3,2,1,0:T(8,128)S(1)}, f32[1,64,32,128]{3,2,1,0:T(8,128)}, u32[]{:S(2)}) copy-start(f32[1,64,32,128]{3,2,1,0:T(8,128)} %param.9) | copy-start | bytes 3145732
  77.9 7.2 %collective-permute-start.12 = (f32[1,32,128]{2,1,0:T(8,128)S(1)}, f32[1,32,128]{2,1,0:T(8,128)S(1)}, u32[]{:S(2)}, u32[]{:S(2)}) collective-permute-start(f32[1,32,128]{2,1,0:T(8,128)S(1)} %get-tuple-element.25), channel_id=1, source_target_pairs={{16,0},{32,16},{48,32},{64,48},{80,64},{96,80},{112,96},{17,1},{33... | collective-permute-start | bytes 49160 | tf_op jit(solution)/shard_map/ppermute | solution.py:118
  79.9 5.3 %collective-permute-start.13 = (f32[1,32,128]{2,1,0:T(8,128)S(1)}, f32[1,32,128]{2,1,0:T(8,128)S(1)}, u32[]{:S(2)}, u32[]{:S(2)}) collective-permute-start(f32[1,32,128]{2,1,0:T(8,128)S(1)} %get-tuple-element.24), channel_id=1, source_target_pairs={{0,16},{16,32},{32,48},{48,64},{64,80},{80,96},{96,112},{1,17},{17... | collective-permute-start | bytes 49160 | tf_op jit(solution)/shard_map/ppermute | solution.py:115
  85.2 5.7 %collective-permute-start.14 = (f32[66,1,128]{2,1,0:T(1,128)S(1)}, f32[66,1,128]{2,1,0:T(1,128)S(1)}, u32[]{:S(2)}, u32[]{:S(2)}) collective-permute-start(f32[66,1,128]{2,1,0:T(1,128)S(1)} %get-tuple-element.14), channel_id=1, source_target_pairs={{1,0},{2,1},{3,2},{4,3},{5,4},{6,5},{7,6},{8,7},{9,8},{10,9},{11,1... | collective-permute-start | bytes 101384 | tf_op jit(solution)/shard_map/ppermute | solution.py:118
  88.4 8.3 %collective-permute-start.15 = (f32[66,1,128]{2,1,0:T(1,128)S(1)}, f32[66,1,128]{2,1,0:T(1,128)S(1)}, u32[]{:S(2)}, u32[]{:S(2)}) collective-permute-start(f32[66,1,128]{2,1,0:T(1,128)S(1)} %get-tuple-element.15), channel_id=1, source_target_pairs={{0,1},{1,2},{2,3},{3,4},{4,5},{5,6},{6,7},{7,8},{8,9},{9,10},{10,1... | collective-permute-start | bytes 101384 | tf_op jit(solution)/shard_map/ppermute | solution.py:115
  98.2 7.1 %collective-permute-start.4 = (f32[1,32,128]{2,1,0:T(8,128)S(1)}, f32[1,32,128]{2,1,0:T(8,128)S(1)}, u32[]{:S(2)}, u32[]{:S(2)}) collective-permute-start(f32[1,32,128]{2,1,0:T(8,128)S(1)} %get-tuple-element.29), channel_id=1, source_target_pairs={{16,0},{32,16},{48,32},{64,48},{80,64},{96,80},{112,96},{17,1},{33... | collective-permute-start | bytes 49160 | tf_op jit(solution)/shard_map/ppermute | solution.py:118
  100.1 5.2 %collective-permute-start.5 = (f32[1,32,128]{2,1,0:T(8,128)S(1)}, f32[1,32,128]{2,1,0:T(8,128)S(1)}, u32[]{:S(2)}, u32[]{:S(2)}) collective-permute-start(f32[1,32,128]{2,1,0:T(8,128)S(1)} %get-tuple-element.28), channel_id=1, source_target_pairs={{0,16},{16,32},{32,48},{48,64},{64,80},{80,96},{96,112},{1,17},{17... | collective-permute-start | bytes 49160 | tf_op jit(solution)/shard_map/ppermute | solution.py:115
  105.4 5.7 %collective-permute-start.6 = (f32[66,1,128]{2,1,0:T(1,128)S(1)}, f32[66,1,128]{2,1,0:T(1,128)S(1)}, u32[]{:S(2)}, u32[]{:S(2)}) collective-permute-start(f32[66,1,128]{2,1,0:T(1,128)S(1)} %get-tuple-element.20), channel_id=1, source_target_pairs={{1,0},{2,1},{3,2},{4,3},{5,4},{6,5},{7,6},{8,7},{9,8},{10,9},{11,1... | collective-permute-start | bytes 101384 | tf_op jit(solution)/shard_map/ppermute | solution.py:118
  107.4 8.3 %collective-permute-start.7 = (f32[66,1,128]{2,1,0:T(1,128)S(1)}, f32[66,1,128]{2,1,0:T(1,128)S(1)}, u32[]{:S(2)}, u32[]{:S(2)}) collective-permute-start(f32[66,1,128]{2,1,0:T(1,128)S(1)} %get-tuple-element.21), channel_id=1, source_target_pairs={{0,1},{1,2},{2,3},{3,4},{4,5},{5,6},{6,7},{7,8},{8,9},{9,10},{10,1... | collective-permute-start | bytes 101384 | tf_op jit(solution)/shard_map/ppermute | solution.py:115
  117.0 11.4 %collective-permute-start.16 = (f32[64,32,128]{2,1,0:T(8,128)S(1)}, f32[64,32,128]{2,1,0:T(8,128)S(1)}, u32[]{:S(2)}, u32[]{:S(2)}) collective-permute-start(f32[64,32,128]{2,1,0:T(8,128)S(1)} %fusion.10), channel_id=1, source_target_pairs={{0,128},{128,0},{1,129},{129,1},{2,130},{130,2},{3,131},{131,3},{4... | collective-permute-start | bytes 3145736 | tf_op jit(solution)/shard_map/ppermute | solution.py:192

commit v3 on v0

v3 whole, which is shorter than its diff:
```python
import functools

import jax
import jax.numpy as jnp
from jax import lax
from jax.experimental import pallas as pl
from jax.experimental.pallas import tpu as pltpu
from jax.sharding import PartitionSpec as P

MESH = pl.DeviceIdType.MESH
step_size = 0.12
TOP = 8
COND, LATE, MIDDLE, START, SECOND = range(5)
X_LOW, X_HIGH, Y_LOW, Y_HIGH = range(4)
CHUNKS = 4
UNROLL = 8


def window_kernel(
    sizes,
    step, holder, cond_in, cool_in, heat_in, late_in, store,
    earliest, mine, theirs, edge_mine, edge_theirs,
    saved, outbox, inbox, cond_raw, late_raw, decay, heat,
    cond, late, middle, start, second,
    cond_x, cond_y, cond_z, late_x, late_y, late_z, middle_x, middle_y, middle_z,
    halo_x, halo_y, pack_y,
    load_sem, own_sem, piece_send, piece_recv, halo_send, halo_recv, core_send, core_recv,
):
    n_tx, n_ty, cells_x, cells_y, cells_z, tiles, rows = sizes
    scen, tx, ty = lax.axis_index("scen"), lax.axis_index("tx"), lax.axis_index("ty")
    me = tx * n_ty + ty
    f32 = jnp.float32

    loads = [
        pltpu.make_async_copy(source, target, load_sem.at[i])
        for i, (source, target) in enumerate(
            [(store, saved), (cond_in, cond_raw), (late_in, late_raw), (cool_in, decay), (heat_in, heat)]
        )
    ]
    for load in loads:
        load.start()

    def device(k):
        t = (me + k) % tiles
        return t, (scen, t // n_ty, t % n_ty)

    other_core = (1 - scen, tx, ty)
    barrier = pltpu.get_barrier_semaphore()

    def greet(k, carry):
        pl.semaphore_signal(barrier, inc=1, device_id=device(k)[1], device_id_type=MESH)
        return carry

    lax.fori_loop(1, tiles, greet, 0)
    pl.semaphore_signal(barrier, inc=1, device_id=other_core, device_id_type=MESH)

    def plane(x):
        return pl.ds(pl.multiple_of(x * cells_y, cells_y), cells_y)

    def piece(t):
        return pl.ds(pl.multiple_of(t * rows, rows), rows)

    here, above, below = pl.ds(TOP, cells_y), pl.ds(TOP + 1, cells_y), pl.ds(TOP - 1, cells_y)
    depth = cond.shape[1]

    def edge_rows(ref, y, first=1):
        flat = ref.reshape(ref.shape[0] * depth, cells_z)
        return flat, pl.ds(first * depth + TOP + y, cells_x, stride=depth)

    there = [tx > 0, tx < n_tx - 1, ty > 0, ty < n_ty - 1]
    neighbour = [(scen, tx - 1, ty), (scen, tx + 1, ty), (scen, tx, ty - 1), (scen, tx, ty + 1)]

    def x_slot(field, side):
        return pl.ds((field * 2 + side) * cells_y, cells_y)

    def y_slot(field, side):
        return pl.ds((field * 2 + side) * cells_x, cells_x)

    def landing(field, side):
        if side < 2:
            return halo_x.at[x_slot(field, side)]
        return halo_y.at[y_slot(field, side - 2)]

    def edge_copy(field, ref, side):
        if side < 2:
            source = ref.at[1 if side == X_LOW else cells_x, here]
        else:
            source = pack_y.at[y_slot(field, side - 2)]
        return pltpu.make_async_remote_copy(
            src_ref=source,
            dst_ref=landing(field, side ^ 1),
            send_sem=halo_send.at[field * 4 + side],
            recv_sem=halo_recv.at[field * 4 + (side ^ 1)],
            device_id=neighbour[side],
            device_id_type=MESH,
        )

    def pack(field, ref):
        for side, y in ((0, 0), (1, cells_y - 1)):
            flat, where = edge_rows(ref, y)
            pack_y[y_slot(field, side), :] = flat[where, :]

    def send_edges(field, ref):
        for side in range(4):
            @pl.when(there[side])
            def _():
                edge_copy(field, ref, side).start()

    def wait_edges(field):
        for side in range(4):
            @pl.when(there[side])
            def _():
                slot = landing(field, side)
                pltpu.make_async_copy(slot, slot, halo_recv.at[field * 4 + side]).wait()

    def unpack(field, ref):
        for side, y in ((0, -1), (1, cells_y)):
            ref[0 if side == 0 else cells_x + 1, here] = halo_x[x_slot(field, side), :]
            flat, where = edge_rows(ref, y)
            flat[where, :] = halo_y[y_slot(field, side), :]

    for side in range(4):
        @pl.when(jnp.logical_not(there[side]))
        def _():
            for field in range(5):
                slot = landing(field, side)
                slot[...] = jnp.zeros(slot.shape, f32)

    def clear(i, carry):
        for ref in (start, second):
            ref[i, pl.ds(0, TOP)] = jnp.zeros((TOP, cells_z), f32)
            ref[i, pl.ds(TOP + cells_y, TOP)] = jnp.zeros((TOP, cells_z), f32)
        return carry

    lax.fori_loop(1, cells_x + 1, clear, 0, unroll=UNROLL)
    for ref in (start, second):
        for i in (0, cells_x + 1):
            ref[i, here] = jnp.zeros((cells_y, cells_z), f32)

    loads[1].wait()
    loads[2].wait()

    def lay(x, carry):
        cond[x + 1, here] = cond_raw[plane(x), :] * (0.5 * step_size)
        late[x + 1, here] = late_raw[plane(x), :]
        return carry

    lax.fori_loop(0, cells_x, lay, 0, unroll=UNROLL)
    pack(COND, cond)
    pack(LATE, late)

    loads[0].wait()
    chosen = step[0]

    def unfold(g, carry):
        for r in range(rows):
            outbox[pl.ds(g * 8 * rows + r, 8, stride=rows), :] = saved[
                chosen, pl.ds(pl.multiple_of(g * 8, 8), 8), pl.ds(r * cells_z, cells_z)
            ]
        return carry

    lax.fori_loop(0, tiles // 8, unfold, 0)
    loads[3].wait()
    loads[4].wait()

    def scale(x, carry):
        decay[plane(x), :] = 1.0 - step_size * decay[plane(x), :]
        heat[plane(x), :] = step_size * heat[plane(x), :]
        return carry

    lax.fori_loop(0, cells_x, scale, 0, unroll=UNROLL)

    pl.semaphore_wait(barrier, tiles)

    send_edges(COND, cond)
    send_edges(LATE, late)

    def send(k, carry):
        t, target = device(k)
        pltpu.make_async_remote_copy(
            src_ref=outbox.at[piece(t)],
            dst_ref=inbox.at[me],
            send_sem=piece_send,
            recv_sem=piece_recv,
            device_id=target,
            device_id_type=MESH,
        ).start()
        return carry

    half = tiles // 2
    lax.fori_loop(1, half, send, 0)
    own = pltpu.make_async_copy(outbox.at[piece(me)], inbox.at[me], own_sem)
    own.start()

    lane = lax.broadcasted_iota(jnp.int32, (cells_y, cells_z), 1)
    inner = jnp.where(lane < cells_z - 1, f32(1), f32(0))
    slope = -0.5 * step_size

    def next_z(value):
        return pltpu.roll(value, cells_z - 1, 1)

    def last_z(value):
        return pltpu.roll(value, 1, 1)

    wait_edges(COND)
    wait_edges(LATE)
    unpack(COND, cond)
    unpack(LATE, late)

    def first_face(ref):
        return ref[1, here] - ref[0, here]

    kx = cond[0, here] + cond[1, here]
    dx = first_face(late)
    cond_x[plane(0), :] = kx
    late_x[plane(0), :] = slope * dx

    def middle_plane(i, carry):
        k, w, flux = carry
        k_next, w_next = cond[i + 1, here], late[i + 1, here]
        kx, dx = k + k_next, w_next - w
        cond_x[plane(i), :] = kx
        late_x[plane(i), :] = slope * dx
        flux_next = kx * dx
        ky_up, ky_down = k + cond[i, above], k + cond[i, below]
        d_up, d_down = late[i, above] - w, w - late[i, below]
        cond_y[i, below] = ky_down
        cond_y[i, here] = ky_up
        late_y[i, below] = slope * d_down
        late_y[i, here] = slope * d_up
        kz, dz = (k + next_z(k)) * inner, next_z(w) - w
        cond_z[plane(i - 1), :] = kz
        late_z[plane(i - 1), :] = dz * (slope * inner)
        fz = kz * dz
        middle[i, here] = (
            decay[plane(i - 1), :] * w
            + (flux_next - flux)
            + (ky_up * d_up - ky_down * d_down)
            + (fz - last_z(fz))
        )
        return k_next, w_next, flux_next

    lax.fori_loop(1, cells_x + 1, middle_plane, (cond[1, here], late[1, here], kx * dx), unroll=UNROLL)
    pack(MIDDLE, middle)
    send_edges(MIDDLE, middle)

    lax.fori_loop(half, tiles, send, 0)

    wait_edges(MIDDLE)
    unpack(MIDDLE, middle)
    dx = first_face(middle)
    middle_x[plane(0), :] = slope * dx

    def earliest_plane(i, carry):
        w, flux = carry
        w_next = middle[i + 1, here]
        dx = w_next - w
        middle_x[plane(i), :] = slope * dx
        flux_next = cond_x[plane(i), :] * dx
        d_up, d_down = middle[i, above] - w, w - middle[i, below]
        middle_y[i, below] = slope * d_down
        middle_y[i, here] = slope * d_up
        dz = next_z(w) - w
        middle_z[plane(i - 1), :] = dz * (slope * inner)
        fz = cond_z[plane(i - 1), :] * dz
        earliest[plane(i - 1), :] = (
            decay[plane(i - 1), :] * w
            + (flux_next - flux)
            + (cond_y[i, here] * d_up - cond_y[i, below] * d_down)
            + (fz - last_z(fz))
        )
        return w_next, flux_next

    lax.fori_loop(1, cells_x + 1, earliest_plane, (middle[1, here], cond_x[plane(0), :] * dx), unroll=UNROLL)

    own.wait()
    received = inbox.at[pl.ds(0, tiles - 1)]
    pltpu.make_async_copy(received, received, piece_recv).wait()
    per_plane = cells_y // rows

    def assemble(x, carry):
        for part in range(per_plane):
            start[x + 1, pl.ds(TOP + part * rows, rows)] = inbox[holder[0, x * per_plane + part]]
        return carry

    lax.fori_loop(0, cells_x, assemble, 0, unroll=UNROLL)
    pack(START, start)
    send_edges(START, start)

    def second_plane(i, carry):
        s, flux, prod = carry
        s_next = start[i + 1, here]
        dx = s_next - s
        flux_next, prod_next = cond_x[plane(i), :] * dx, middle_x[plane(i), :] * dx
        d_up, d_down = start[i, above] - s, s - start[i, below]
        dz = next_z(s) - s
        fz, pz = cond_z[plane(i - 1), :] * dz, middle_z[plane(i - 1), :] * dz
        second[i, here] = (
            (decay[plane(i - 1), :] * s + heat[plane(i - 1), :])
            + (flux_next - flux)
            + (cond_y[i, here] * d_up - cond_y[i, below] * d_down)
            + (fz - last_z(fz))
        )
        mine[plane(i - 1), :] = (
            (prod_next + prod)
            + (middle_y[i, here] * d_up + middle_y[i, below] * d_down)
            + (pz + last_z(pz))
        )
        return s_next, flux_next, prod_next

    s = start[1, here]
    lax.fori_loop(1, cells_x + 1, second_plane, (s, cond_x[plane(0), :] * s, middle_x[plane(0), :] * s), unroll=UNROLL)

    wait_edges(START)
    for side, y, face in ((0, 0, -1), (1, cells_y - 1, cells_y - 1)):
        x = 0 if side == 0 else cells_x - 1
        second[x + 1, here] = (
            second[x + 1, here] + cond_x[plane(x + side), :] * halo_x[x_slot(START, side), :]
        )
        flat, where = edge_rows(second, y)
        faces, at = edge_rows(cond_y, face)
        flat[where, :] = flat[where, :] + faces[at, :] * halo_y[y_slot(START, side), :]
    pack(SECOND, second)
    send_edges(SECOND, second)

    def late_plane(i, carry):
        s, prod = carry
        s_next = second[i + 1, here]
        prod_next = late_x[plane(i), :] * (s_next - s)
        d_up, d_down = second[i, above] - s, s - second[i, below]
        pz = late_z[plane(i - 1), :] * (next_z(s) - s)
        mine[plane(i - 1), :] = (
            mine[plane(i - 1), :]
            + (prod_next + prod)
            + (late_y[i, here] * d_up + late_y[i, below] * d_down)
            + (pz + last_z(pz))
        )
        return s_next, prod_next

    def core_copy(index, source, target):
        return pltpu.make_async_remote_copy(
            src_ref=source,
            dst_ref=target,
            send_sem=core_send.at[index],
            recv_sem=core_recv.at[index],
            device_id=other_core,
            device_id_type=MESH,
        )

    chunk = cells_x // CHUNKS
    s = second[1, here]
    carry = (s, late_x[plane(0), :] * s)
    crossing = []
    for c in range(CHUNKS):
        carry = lax.fori_loop(1 + c * chunk, 1 + (c + 1) * chunk, late_plane, carry, unroll=UNROLL)
        part = pl.ds(c * chunk * cells_y, chunk * cells_y)
        crossing.append(core_copy(c, mine.at[part], theirs.at[part]))
        crossing[-1].start()

    wait_edges(SECOND)
    for side, face, sign in ((0, -1, -1.0), (1, cells_y - 1, 1.0)):
        x = 0 if side == 0 else cells_x
        edge_mine[pl.ds(side * cells_y, cells_y), :] = sign * (
            middle_x[plane(x), :] * halo_x[x_slot(START, side), :]
            + late_x[plane(x), :] * halo_x[x_slot(SECOND, side), :]
        )
        early, where = edge_rows(middle_y, face)
        lately, at = edge_rows(late_y, face)
        edge_mine[pl.ds(2 * cells_y + side * cells_x, cells_x), :] = sign * (
            early[where, :] * halo_y[y_slot(START, side), :]
            + lately[at, :] * halo_y[y_slot(SECOND, side), :]
        )
    crossing.append(core_copy(CHUNKS, edge_mine, edge_theirs))
    crossing[-1].start()

    sent = outbox.at[pl.ds(0, (tiles - 1) * rows)]
    pltpu.make_async_copy(sent, sent, piece_send).wait()
    for field, ref in enumerate((cond, late, middle, start, second)):
        for side in range(4):
            @pl.when(there[side])
            def _():
                edge_copy(field, ref, side).wait_send()
    for copy in crossing:
        copy.wait()


def finish_kernel(sizes, earliest, mine, theirs, edge_mine, edge_theirs, adjoint_out, gradient, total, copy_sem, part_sem):
    cells_x, cells_y = sizes
    whole = pltpu.make_async_copy(earliest, adjoint_out, copy_sem)
    whole.start()
    edge = 2 * cells_y
    chunk = cells_x // CHUNKS
    copies = []
    for c in range(CHUNKS):
        part = pl.ds(c * chunk * cells_y, chunk * cells_y)
        total[part, :] = mine[part, :] + theirs[part, :]
        for side in range(2):
            if c == side * (CHUNKS - 1):
                here = pl.ds(side * (cells_x - 1) * cells_y, cells_y)
                added = pl.ds(side * cells_y, cells_y)
                total[here, :] = total[here, :] + (edge_mine[added, :] + edge_theirs[added, :])
            here = pl.ds(c * chunk * cells_y + side * (cells_y - 1), chunk, stride=cells_y)
            added = pl.ds(edge + side * cells_x + c * chunk, chunk)
            total[here, :] = total[here, :] + (edge_mine[added, :] + edge_theirs[added, :])
        copies.append(pltpu.make_async_copy(total.at[part], gradient.at[part], part_sem.at[c]))
        copies[-1].start()
    whole.wait()
    for copy in copies:
        copy.wait()


def local(n_tx, n_ty, conductivity, cooling, source, adjoint_in, store, holder, step_index):
    cells_x, cells_y, cells_z = conductivity.shape
    _, held, _, tiles, piece = store.shape
    rows = piece // cells_z
    sizes = (n_tx, n_ty, cells_x, cells_y, cells_z, tiles, rows)
    flat = (cells_x * cells_y, cells_z)
    faces = ((cells_x + 1) * cells_y, cells_z)
    padded = (cells_x + 2, 2 * TOP + cells_y, cells_z)
    edges = (2 * cells_y + 2 * cells_x, cells_z)
    f32 = jnp.float32

    def vmem(shape):
        return pltpu.VMEM(shape, f32)

    in_smem = pl.BlockSpec(memory_space=pltpu.SMEM)
    in_hbm = pl.BlockSpec(memory_space=pltpu.HBM)
    in_vmem = pl.BlockSpec(memory_space=pltpu.VMEM)
    shaped = jax.ShapeDtypeStruct
    results = pl.pallas_call(
        functools.partial(window_kernel, sizes),
        out_shape=[shaped(flat, f32)] * 3 + [shaped(edges, f32)] * 2,
        in_specs=[in_smem] * 2 + [in_hbm] * 5,
        out_specs=[in_vmem] * 5,
        scratch_shapes=[
            vmem((held, tiles, piece)),
            vmem(flat),
            vmem((tiles, rows, cells_z)),
            *[vmem(flat)] * 4,
            *[vmem(padded)] * 5,
            *[vmem(faces), vmem(padded), vmem(flat)] * 3,
            vmem((10 * cells_y, cells_z)),
            *[vmem((10 * cells_x, cells_z))] * 2,
            pltpu.SemaphoreType.DMA((5,)),
            *[pltpu.SemaphoreType.DMA] * 3,
            *[pltpu.SemaphoreType.DMA((20,))] * 2,
            *[pltpu.SemaphoreType.DMA((CHUNKS + 1,))] * 2,
        ],
        compiler_params=pltpu.CompilerParams(
            collective_id=0, has_side_effects=True, vmem_limit_bytes=50 << 20
        ),
    )(
        step_index,
        holder,
        conductivity.reshape(flat),
        cooling.reshape(flat),
        source.reshape(flat),
        adjoint_in.reshape(flat),
        store.reshape(held, tiles, piece),
    )
    adjoint_out, gradient = pl.pallas_call(
        functools.partial(finish_kernel, (cells_x, cells_y)),
        out_shape=[shaped(flat, f32)] * 2,
        in_specs=[in_vmem] * 5,
        out_specs=[in_hbm] * 2,
        scratch_shapes=[vmem(flat), pltpu.SemaphoreType.DMA, pltpu.SemaphoreType.DMA((CHUNKS,))],
        compiler_params=pltpu.CompilerParams(vmem_limit_bytes=4 << 20),
    )(*results)
    return adjoint_out.reshape(adjoint_in.shape), gradient.reshape(conductivity.shape)


def solution(mesh):
    in_specs = (
        P("tx", "ty", None),
        P("scen", "tx", "ty", None),
        P("scen", "tx", "ty", None),
        P("scen", "tx", "ty", None),
        P("scen", None, ("tx", "ty"), None, None),
        P(("tx", "ty"), None),
        P("scen"),
    )
    out_specs = (P("scen", "tx", "ty", None), P("tx", "ty", None))
    body = functools.partial(local, mesh.shape["tx"], mesh.shape["ty"])
    return jax.shard_map(body, mesh=mesh, in_specs=in_specs, out_specs=out_specs, check_vma=False)
```

time: 170 us -> 55.3 us (0.33); the launches traced: 168 us -> 55.2 us
  starting transfers between devices: 65.5 us -> 0 us
  waiting for transfers between devices: 56 us -> 0 us
  Pallas kernels: 0 us -> 53.3 us
  other arithmetic: 16.3 us -> 0 us
  local copies, waits for them, and re-layouts: 14.8 us -> 0.65 us
  between operations: 15.2 us -> 1.29 us
    pallas_call x0 -> x2, Pallas kernels: none -> 53.3 us  [the longest x1 52 us: local(): pl.pallas_call(functools.partial(window_kernel, sizes), out_shape=[shaped...]
    ppermute x16 -> x0, starting transfers between devices: 50 us -> none  [the longest x8 27.9 us: padded_2(): lax.ppermute(lax.slice_in_dim(block, block.shape[dim] - width, None, axis...]
    psum x1 -> x0, waiting for transfers between devices: 33 us -> none  [local(): summed = lax.psum(gradient, 'scen')]
    ppermute x16 -> x0, waiting for transfers between devices: 22.8 us -> none  [the longest x8 20.2 us: padded_2(): lax.ppermute(lax.slice_in_dim(block, block.shape[dim] - width, None, axis...]
    all_to_all x1 -> x0, starting transfers between devices: 15.4 us -> none  [local(): lax.all_to_all(chosen, ('tx', 'ty'), split_axis=0, concat_axis=0, tiled=T...]
    mul x10 -> x0, other arithmetic: 7.87 us -> none  [the longest x2 2.92 us: face_products(): (inner_state[:, :, 1:] - inner_state[:, :, :-1]) * (inner_adjoint[:, :, 1...]
    unnamed x25 -> x2, local copies, waits for them, and re-layouts: 5.75 us -> 0.65 us
    gather x2 -> x0, local copies, waits for them, and re-layouts: 4.36 us -> none  [local(): jnp.take(arrived, holder[0], axis=0).reshape(cells_x, cells_y, cells_z)]
  transfers between devices with their start and end apart: 18 -> 0, of which waited for: 7 -> 0; matrix products, arithmetic and copies ran while one was open for 8% -> 0% of each run, Pallas kernels for 0% -> 0%
where the time goes in v3:
time: 55.3 us; the launch traced here: 55.2 us
  Pallas kernels  53.3 us (96%)
  between operations  1.29 us (2%)
  local copies, waits for them, and re-layouts  0.65 us (1%)
    pallas_call x1, Pallas kernels, local(): pl.pallas_call(functools.partial(window_kernel, sizes), out_shape=[shaped...  52 us
    pallas_call x1, Pallas kernels, local(): pl.pallas_call(functools.partial(finish_kernel, (cells_x, cells_y)), out_...  1.35 us

profile of v3, /device:TPU:7, one launch (start us, length us, event | category | flops | bytes accessed | tf_op | source)
XLA Modules:
  0.0 55.2 jit_solution(6948533563901707510)
XLA Ops:
  1.3 0.0 copy-start
  1.3 0.6 %copy-done = s32[1,128]{1,0:T(1,128)S(1)} copy-done((s32[1,128]{1,0:T(1,128)S(1)}, s32[1,128]{1,0:T(1,128)}, u32[]{:S(2)}) %copy-start) | copy-done | bytes 536
  1.9 52.0 %shard_map.86 = (f32[2048,128]{1,0:T(8,128)S(1)}, f32[2048,128]{1,0:T(8,128)S(1)}, f32[2048,128]{1,0:T(8,128)S(1)}, f32[192,128]{1,0:T(8,128)S(1)}, f32[192,128]{1,0:T(8,128)S(1)}) custom-call(s32[1]{0:T(128)S(6)} %copy.9.step, s32[1,128]{1,0:T(1,128)S(1)} %copy-done, f32[2048,128]{1,0:T(8,128)} %bitcast.8, f32[2048,128]{1,0:T(8,128)} %bitcast.9, ...), custom_call_target="tpu_custom_call" | custom-call | tf_op jit(solution)/shard_map/pallas_call | solution.py:430
  53.9 1.4 %shard_map.87 = (f32[2048,128]{1,0:T(8,128)}, f32[2048,128]{1,0:T(8,128)}) custom-call(f32[2048,128]{1,0:T(8,128)S(1)} %get-tuple-element.9.earliest, f32[2048,128]{1,0:T(8,128)S(1)} %get-tuple-element.10.mine, f32[2048,128]{1,0:T(8,128)S(1)} %get-tuple-element.11.theirs, f32[192,128]{1,0:T(8,128)S(1)} %get-tuple-element.12.edge_mine, ...), custom_call_target="tpu_custom_call" | custom-call | tf_op jit(solution)/shard_map/pallas_call | solution.py:461
Async XLA Ops:
  1.3 0.7 %copy-start = (s32[1,128]{1,0:T(1,128)S(1)}, s32[1,128]{1,0:T(1,128)}, u32[]{:S(2)}) copy-start(s32[1,128]{1,0:T(1,128)} %holder.1) | copy-start | bytes 1540

commit v4 on v3

--- a/solution.py
+++ b/solution.py
@@ -18,9 +18,9 @@
 
 def window_kernel(
     sizes,
-    step, holder, cond_in, cool_in, heat_in, late_in, store,
+    step_in, holder_in, cond_in, cool_in, heat_in, late_in, store,
     earliest, mine, theirs, edge_mine, edge_theirs,
-    saved, outbox, inbox, cond_raw, late_raw, decay, heat,
+    step, holder, saved, outbox, inbox, cond_raw, late_raw, decay, heat,
     cond, late, middle, start, second,
     cond_x, cond_y, cond_z, late_x, late_y, late_z, middle_x, middle_y, middle_z,
     halo_x, halo_y, pack_y,
@@ -34,7 +34,15 @@
     loads = [
         pltpu.make_async_copy(source, target, load_sem.at[i])
         for i, (source, target) in enumerate(
-            [(store, saved), (cond_in, cond_raw), (late_in, late_raw), (cool_in, decay), (heat_in, heat)]
+            [
+                (step_in, step),
+                (store, saved),
+                (cond_in, cond_raw),
+                (late_in, late_raw),
+                (cool_in, decay),
+                (heat_in, heat),
+                (holder_in, holder),
+            ]
         )
     ]
     for load in loads:
@@ -51,7 +59,7 @@
         pl.semaphore_signal(barrier, inc=1, device_id=device(k)[1], device_id_type=MESH)
         return carry
 
-    lax.fori_loop(1, tiles, greet, 0)
+    lax.fori_loop(1, tiles, greet, 0, unroll=True)
     pl.semaphore_signal(barrier, inc=1, device_id=other_core, device_id_type=MESH)
 
     def plane(x):
@@ -137,8 +145,8 @@
         for i in (0, cells_x + 1):
             ref[i, here] = jnp.zeros((cells_y, cells_z), f32)
 
-    loads[1].wait()
     loads[2].wait()
+    loads[3].wait()
 
     def lay(x, carry):
         cond[x + 1, here] = cond_raw[plane(x), :] * (0.5 * step_size)
@@ -150,6 +158,8 @@
     pack(LATE, late)
 
     loads[0].wait()
+    loads[1].wait()
+    loads[6].wait()
     chosen = step[0]
 
     def unfold(g, carry):
@@ -160,8 +170,8 @@
         return carry
 
     lax.fori_loop(0, tiles // 8, unfold, 0)
-    loads[3].wait()
     loads[4].wait()
+    loads[5].wait()
 
     def scale(x, carry):
         decay[plane(x), :] = 1.0 - step_size * decay[plane(x), :]
@@ -423,16 +433,17 @@
     def vmem(shape):
         return pltpu.VMEM(shape, f32)
 
-    in_smem = pl.BlockSpec(memory_space=pltpu.SMEM)
     in_hbm = pl.BlockSpec(memory_space=pltpu.HBM)
     in_vmem = pl.BlockSpec(memory_space=pltpu.VMEM)
     shaped = jax.ShapeDtypeStruct
     results = pl.pallas_call(
         functools.partial(window_kernel, sizes),
         out_shape=[shaped(flat, f32)] * 3 + [shaped(edges, f32)] * 2,
-        in_specs=[in_smem] * 2 + [in_hbm] * 5,
+        in_specs=[in_hbm] * 7,
         out_specs=[in_vmem] * 5,
         scratch_shapes=[
+            pltpu.SMEM(step_index.shape, jnp.int32),
+            pltpu.SMEM(holder.shape, jnp.int32),
             vmem((held, tiles, piece)),
             vmem(flat),
             vmem((tiles, rows, cells_z)),
@@ -441,7 +452,7 @@
             *[vmem(faces), vmem(padded), vmem(flat)] * 3,
             vmem((10 * cells_y, cells_z)),
             *[vmem((10 * cells_x, cells_z))] * 2,
-            pltpu.SemaphoreType.DMA((5,)),
+            pltpu.SemaphoreType.DMA((7,)),
             *[pltpu.SemaphoreType.DMA] * 3,
             *[pltpu.SemaphoreType.DMA((20,))] * 2,
             *[pltpu.SemaphoreType.DMA((CHUNKS + 1,))] * 2,

time: 55.3 us -> 54.3 us (0.982)
  Pallas kernels: 53.3 us -> 52.3 us
    pallas_call x1, Pallas kernels: 52 us -> 50.9 us  [local(): pl.pallas_call(functools.partial(window_kernel, sizes), out_shape=[shaped...]
where the time goes in v4:
time: 54.3 us; the launch traced here: 54.2 us
  Pallas kernels  52.3 us (96%)
  between operations  1.29 us (2%)
  local copies, waits for them, and re-layouts  0.65 us (1%)
    pallas_call x1, Pallas kernels, local(): pl.pallas_call(functools.partial(window_kernel, sizes), out_shape=[shaped...  50.9 us
    pallas_call x1, Pallas kernels, local(): pl.pallas_call(functools.partial(finish_kernel, (cells_x, cells_y)), out_...  1.35 us

profile of v4, /device:TPU:7, one launch (start us, length us, event | category | flops | bytes accessed | tf_op | source)
XLA Modules:
  0.0 54.2 jit_solution(11765043365385852935)
XLA Ops:
  1.3 0.0 copy-start
  1.3 0.6 %copy-done = s32[1,128]{1,0:T(1,128)S(1)} copy-done((s32[1,128]{1,0:T(1,128)S(1)}, s32[1,128]{1,0:T(1,128)}, u32[]{:S(2)}) %copy-start) | copy-done | bytes 536
  1.9 50.9 %shard_map.86 = (f32[2048,128]{1,0:T(8,128)S(1)}, f32[2048,128]{1,0:T(8,128)S(1)}, f32[2048,128]{1,0:T(8,128)S(1)}, f32[192,128]{1,0:T(8,128)S(1)}, f32[192,128]{1,0:T(8,128)S(1)}) custom-call(s32[1]{0:T(128)S(6)} %copy.9.step_in, s32[1,128]{1,0:T(1,128)S(1)} %copy-done, f32[2048,128]{1,0:T(8,128)} %bitcast.8, f32[2048,128]{1,0:T(8,128)} %bitcast.9, ...), custom_call_target="tpu_custom_call" | custom-call | tf_op jit(solution)/shard_map/pallas_call | solution.py:439
  52.9 1.4 %shard_map.87 = (f32[2048,128]{1,0:T(8,128)}, f32[2048,128]{1,0:T(8,128)}) custom-call(f32[2048,128]{1,0:T(8,128)S(1)} %get-tuple-element.9.earliest, f32[2048,128]{1,0:T(8,128)S(1)} %get-tuple-element.10.mine, f32[2048,128]{1,0:T(8,128)S(1)} %get-tuple-element.11.theirs, f32[192,128]{1,0:T(8,128)S(1)} %get-tuple-element.12.edge_mine, ...), custom_call_target="tpu_custom_call" | custom-call | tf_op jit(solution)/shard_map/pallas_call | solution.py:472
Async XLA Ops:
  1.3 0.7 %copy-start = (s32[1,128]{1,0:T(1,128)S(1)}, s32[1,128]{1,0:T(1,128)}, u32[]{:S(2)}) copy-start(s32[1,128]{1,0:T(1,128)} %holder_in.1) | copy-start | bytes 1540

commit v5 on v4

--- a/solution.py
+++ b/solution.py
@@ -23,7 +23,7 @@
     step, holder, saved, outbox, inbox, cond_raw, late_raw, decay, heat,
     cond, late, middle, start, second,
     cond_x, cond_y, cond_z, late_x, late_y, late_z, middle_x, middle_y, middle_z,
-    halo_x, halo_y, pack_y,
+    halo_x, halo_y, halo_corner, pack_x, pack_y, pack_corner, shift_x, shift_y,
     load_sem, own_sem, piece_send, piece_recv, halo_send, halo_recv, core_send, core_recv,
 ):
     n_tx, n_ty, cells_x, cells_y, cells_z, tiles, rows = sizes
@@ -90,7 +90,9 @@
         return halo_y.at[y_slot(field, side - 2)]
 
     def edge_copy(field, ref, side):
-        if side < 2:
+        if side < 2 and field == SECOND:
+            source = pack_x.at[pl.ds(side * cells_y, cells_y)]
+        elif side < 2:
             source = ref.at[1 if side == X_LOW else cells_x, here]
         else:
             source = pack_y.at[y_slot(field, side - 2)]
@@ -114,6 +116,23 @@
             def _():
                 edge_copy(field, ref, side).start()
 
+    corners = [(0, 0), (0, 1), (1, 0), (1, 1)]
+    beyond = [jnp.logical_and(there[i], there[2 + j]) for i, j in corners]
+
+    def corner_rows(c):
+        return pl.ds(c * 8, 8)
+
+    def corner_copy(c):
+        i, j = corners[c]
+        return pltpu.make_async_remote_copy(
+            src_ref=pack_corner.at[corner_rows(c)],
+            dst_ref=halo_corner.at[corner_rows(3 - c)],
+            send_sem=halo_send.at[20 + c],
+            recv_sem=halo_recv.at[20 + 3 - c],
+            device_id=(scen, tx + 2 * i - 1, ty + 2 * j - 1),
+            device_id_type=MESH,
+        )
+
     def wait_edges(field):
         for side in range(4):
             @pl.when(there[side])
@@ -133,6 +152,15 @@
             for field in range(5):
                 slot = landing(field, side)
                 slot[...] = jnp.zeros(slot.shape, f32)
+
+    for c in range(4):
+        @pl.when(jnp.logical_not(beyond[c]))
+        def _():
+            halo_corner[corner_rows(c), :] = jnp.zeros((8, cells_z), f32)
+
+    pack_corner[...] = jnp.zeros(pack_corner.shape, f32)
+    shift_x[...] = jnp.zeros(shift_x.shape, f32)
+    shift_y[...] = jnp.zeros(shift_y.shape, f32)
 
     def clear(i, carry):
         for ref in (start, second):
@@ -297,6 +325,45 @@
     pack(START, start)
     send_edges(START, start)
 
+    def row(ref, y, first=1):
+        flat, where = edge_rows(ref, y, first)
+        return flat[where, :]
+
+    def flat_row(ref, y, first=0):
+        return ref[pl.ds(first * cells_y + y, cells_x, stride=cells_y), :]
+
+    def advanced(s, x_next, x_last, y_next, y_last, kx_next, kx_last, ky_next, ky_last, kz, a, b):
+        fz = kz * (next_z(s) - s)
+        return (
+            (a * s + b)
+            + (kx_next * (x_next - s) - kx_last * (s - x_last))
+            + (ky_next * (y_next - s) - ky_last * (s - y_last))
+            + (fz - last_z(fz))
+        )
+
+    for side, i, y in ((0, 1, 0), (1, cells_x, cells_y - 1)):
+        at = plane(i - 1)
+        pack_x[pl.ds(side * cells_y, cells_y), :] = advanced(
+            start[i, here], start[i + 1, here], start[i - 1, here], start[i, above], start[i, below],
+            cond_x[plane(i), :], cond_x[at, :], cond_y[i, here], cond_y[i, below],
+            cond_z[at, :], decay[at, :], heat[at, :],
+        )
+        pack_y[y_slot(SECOND, side), :] = advanced(
+            row(start, y), row(start, y, 2), row(start, y, 0), row(start, y + 1), row(start, y - 1),
+            flat_row(cond_x, y, 1), flat_row(cond_x, y), row(cond_y, y), row(cond_y, y - 1),
+            flat_row(cond_z, y), flat_row(decay, y), flat_row(heat, y),
+        )
+    for c, (i, j) in enumerate(corners):
+        x, y = i * (cells_x - 1), j * (cells_y - 1)
+        value = start[x + 1, pl.ds(TOP + y, 1)]
+        pack_corner[pl.ds(c * 8, 1), :] = value * cond_y[x + 1, pl.ds(TOP + y - 1 + j, 1)]
+        pack_corner[pl.ds(c * 8 + 1, 1), :] = value * cond_x[pl.ds((x + i) * cells_y + y, 1), :]
+    send_edges(SECOND, second)
+    for c in range(4):
+        @pl.when(beyond[c])
+        def _():
+            corner_copy(c).start()
+
     def second_plane(i, carry):
         s, flux, prod = carry
         s_next = start[i + 1, here]
@@ -321,18 +388,6 @@
     s = start[1, here]
     lax.fori_loop(1, cells_x + 1, second_plane, (s, cond_x[plane(0), :] * s, middle_x[plane(0), :] * s), unroll=UNROLL)
 
-    wait_edges(START)
-    for side, y, face in ((0, 0, -1), (1, cells_y - 1, cells_y - 1)):
-        x = 0 if side == 0 else cells_x - 1
-        second[x + 1, here] = (
-            second[x + 1, here] + cond_x[plane(x + side), :] * halo_x[x_slot(START, side), :]
-        )
-        flat, where = edge_rows(second, y)
-        faces, at = edge_rows(cond_y, face)
-        flat[where, :] = flat[where, :] + faces[at, :] * halo_y[y_slot(START, side), :]
-    pack(SECOND, second)
-    send_edges(SECOND, second)
-
     def late_plane(i, carry):
         s, prod = carry
         s_next = second[i + 1, here]
@@ -367,19 +422,63 @@
         crossing.append(core_copy(c, mine.at[part], theirs.at[part]))
         crossing[-1].start()
 
+    wait_edges(START)
     wait_edges(SECOND)
-    for side, face, sign in ((0, -1, -1.0), (1, cells_y - 1, 1.0)):
-        x = 0 if side == 0 else cells_x
-        edge_mine[pl.ds(side * cells_y, cells_y), :] = sign * (
-            middle_x[plane(x), :] * halo_x[x_slot(START, side), :]
-            + late_x[plane(x), :] * halo_x[x_slot(SECOND, side), :]
-        )
-        early, where = edge_rows(middle_y, face)
-        lately, at = edge_rows(late_y, face)
-        edge_mine[pl.ds(2 * cells_y + side * cells_x, cells_x), :] = sign * (
-            early[where, :] * halo_y[y_slot(START, side), :]
-            + lately[at, :] * halo_y[y_slot(SECOND, side), :]
-        )
+    for c in range(4):
+        @pl.when(beyond[c])
+        def _():
+            slot = halo_corner.at[corner_rows(c)]
+            pltpu.make_async_copy(slot, slot, halo_recv.at[20 + c]).wait()
+
+    known = [jnp.where(exists, f32(1), f32(0)) for exists in there]
+
+    def added(add, add_next, add_last, inner_last, inner_next, up, down, z):
+        pz = z * (next_z(add) - add)
+        return (
+            add * (inner_last - inner_next)
+            + (up * (add_next - add) + down * (add - add_last))
+            + (pz + last_z(pz))
+        )
+
+    for side, sign in ((0, -1.0), (1, 1.0)):
+        i, face, inward = (1, 0, 1) if side == 0 else (cells_x, cells_x, cells_x - 1)
+        near = x_slot(START, side)
+        far = x_slot(SECOND, side)
+        k = cond_x[plane(face), :]
+        add = k * halo_x[near, :]
+        halo_x[far, :] = halo_x[far, :] + known[side] * (k * start[i, here])
+        for j in range(2):
+            at = pl.ds((SECOND * 2 + side) * cells_y + j * (cells_y - 1), 1)
+            halo_x[at, :] = halo_x[at, :] + halo_corner[pl.ds((side * 2 + j) * 8, 1), :]
+        base = side * (cells_y + 2 * TOP) + TOP
+        shift_x[pl.ds(base, cells_y), :] = add
+        edge_mine[pl.ds(side * cells_y, cells_y), :] = added(
+            add, shift_x[pl.ds(base + 1, cells_y), :], shift_x[pl.ds(base - 1, cells_y), :],
+            late_x[plane(i - 1), :], late_x[plane(i), :],
+            late_y[i, here], late_y[i, below], late_z[plane(i - 1), :],
+        ) + sign * (
+            middle_x[plane(face), :] * halo_x[near, :] + late_x[plane(face), :] * halo_x[far, :]
+        )
+        edge_mine[pl.ds((2 + side) * cells_y, cells_y), :] = sign * (add * late_x[plane(inward), :])
+
+        y, face, inward = (0, -1, 0) if side == 0 else (cells_y - 1, cells_y - 1, cells_y - 2)
+        near = y_slot(START, side)
+        far = y_slot(SECOND, side)
+        k = row(cond_y, face)
+        add = k * halo_y[near, :]
+        halo_y[far, :] = halo_y[far, :] + known[2 + side] * (k * row(start, y))
+        for j in range(2):
+            at = pl.ds((SECOND * 2 + side) * cells_x + j * (cells_x - 1), 1)
+            halo_y[at, :] = halo_y[at, :] + halo_corner[pl.ds((j * 2 + side) * 8 + 1, 1), :]
+        base = side * (cells_x + 2 * TOP) + TOP
+        shift_y[pl.ds(base, cells_x), :] = add
+        edges_y = 4 * cells_y + side * cells_x
+        edge_mine[pl.ds(edges_y, cells_x), :] = added(
+            add, shift_y[pl.ds(base + 1, cells_x), :], shift_y[pl.ds(base - 1, cells_x), :],
+            row(late_y, y - 1), row(late_y, y),
+            flat_row(late_x, y, 1), flat_row(late_x, y), flat_row(late_z, y),
+        ) + sign * (row(middle_y, face) * halo_y[near, :] + row(late_y, face) * halo_y[far, :])
+        edge_mine[pl.ds(edges_y + 2 * cells_x, cells_x), :] = sign * (add * row(late_y, inward))
     crossing.append(core_copy(CHUNKS, edge_mine, edge_theirs))
     crossing[-1].start()
 
@@ -390,6 +489,10 @@
             @pl.when(there[side])
             def _():
                 edge_copy(field, ref, side).wait_send()
+    for c in range(4):
+        @pl.when(beyond[c])
+        def _():
+            corner_copy(c).wait_send()
     for copy in crossing:
         copy.wait()
 
@@ -398,20 +501,22 @@
     cells_x, cells_y = sizes
     whole = pltpu.make_async_copy(earliest, adjoint_out, copy_sem)
     whole.start()
-    edge = 2 * cells_y
     chunk = cells_x // CHUNKS
     copies = []
     for c in range(CHUNKS):
         part = pl.ds(c * chunk * cells_y, chunk * cells_y)
         total[part, :] = mine[part, :] + theirs[part, :]
-        for side in range(2):
-            if c == side * (CHUNKS - 1):
-                here = pl.ds(side * (cells_x - 1) * cells_y, cells_y)
-                added = pl.ds(side * cells_y, cells_y)
+        for depth in range(2):
+            for side in range(2):
+                if c == side * (CHUNKS - 1):
+                    x = cells_x - 1 - depth if side else depth
+                    here = pl.ds(x * cells_y, cells_y)
+                    added = pl.ds((2 * depth + side) * cells_y, cells_y)
+                    total[here, :] = total[here, :] + (edge_mine[added, :] + edge_theirs[added, :])
+                y = cells_y - 1 - depth if side else depth
+                here = pl.ds(c * chunk * cells_y + y, chunk, stride=cells_y)
+                added = pl.ds(4 * cells_y + (2 * depth + side) * cells_x + c * chunk, chunk)
                 total[here, :] = total[here, :] + (edge_mine[added, :] + edge_theirs[added, :])
-            here = pl.ds(c * chunk * cells_y + side * (cells_y - 1), chunk, stride=cells_y)
-            added = pl.ds(edge + side * cells_x + c * chunk, chunk)
-            total[here, :] = total[here, :] + (edge_mine[added, :] + edge_theirs[added, :])
         copies.append(pltpu.make_async_copy(total.at[part], gradient.at[part], part_sem.at[c]))
         copies[-1].start()
     whole.wait()
@@ -427,7 +532,7 @@
     flat = (cells_x * cells_y, cells_z)
     faces = ((cells_x + 1) * cells_y, cells_z)
     padded = (cells_x + 2, 2 * TOP + cells_y, cells_z)
-    edges = (2 * cells_y + 2 * cells_x, cells_z)
+    edges = (4 * cells_y + 4 * cells_x, cells_z)
     f32 = jnp.float32
 
     def vmem(shape):
@@ -451,10 +556,16 @@
             *[vmem(padded)] * 5,
             *[vmem(faces), vmem(padded), vmem(flat)] * 3,
             vmem((10 * cells_y, cells_z)),
-            *[vmem((10 * cells_x, cells_z))] * 2,
+            vmem((10 * cells_x, cells_z)),
+            vmem((32, cells_z)),
+            vmem((2 * cells_y, cells_z)),
+            vmem((10 * cells_x, cells_z)),
+            vmem((32, cells_z)),
+            vmem((2 * (cells_y + 2 * TOP), cells_z)),
+            vmem((2 * (cells_x + 2 * TOP), cells_z)),
             pltpu.SemaphoreType.DMA((7,)),
             *[pltpu.SemaphoreType.DMA] * 3,
-            *[pltpu.SemaphoreType.DMA((20,))] * 2,
+            *[pltpu.SemaphoreType.DMA((24,))] * 2,
             *[pltpu.SemaphoreType.DMA((CHUNKS + 1,))] * 2,
         ],
         compiler_params=pltpu.CompilerParams(

time: 54.3 us -> 51.6 us (0.950)
  Pallas kernels: 52.3 us -> 49.6 us
    pallas_call x1, Pallas kernels: 50.9 us -> 48.2 us  [local(): pl.pallas_call(functools.partial(window_kernel, sizes), out_shape=[shaped...]
where the time goes in v5:
time: 51.6 us; the launch traced here: 51.5 us
  Pallas kernels  49.6 us (96%)
  between operations  1.29 us (2%)
  local copies, waits for them, and re-layouts  0.65 us (1%)
    pallas_call x1, Pallas kernels, local(): pl.pallas_call(functools.partial(window_kernel, sizes), out_shape=[shaped...  48.2 us
    pallas_call x1, Pallas kernels, local(): pl.pallas_call(functools.partial(finish_kernel, (cells_x, cells_y)), out_...  1.35 us

profile of v5, /device:TPU:7, one launch (start us, length us, event | category | flops | bytes accessed | tf_op | source)
XLA Modules:
  0.0 51.5 jit_solution(17840872924946739587)
XLA Ops:
  1.3 0.0 copy-start
  1.3 0.6 %copy-done = s32[1,128]{1,0:T(1,128)S(1)} copy-done((s32[1,128]{1,0:T(1,128)S(1)}, s32[1,128]{1,0:T(1,128)}, u32[]{:S(2)}) %copy-start) | copy-done | bytes 536
  1.9 48.2 %shard_map.86 = (f32[2048,128]{1,0:T(8,128)S(1)}, f32[2048,128]{1,0:T(8,128)S(1)}, f32[2048,128]{1,0:T(8,128)S(1)}, f32[384,128]{1,0:T(8,128)S(1)}, f32[384,128]{1,0:T(8,128)S(1)}) custom-call(s32[1]{0:T(128)S(6)} %copy.9.step_in, s32[1,128]{1,0:T(1,128)S(1)} %copy-done, f32[2048,128]{1,0:T(8,128)} %bitcast.8, f32[2048,128]{1,0:T(8,128)} %bitcast.9, ...), custom_call_target="tpu_custom_call" | custom-call | tf_op jit(solution)/shard_map/pallas_call | solution.py:544
  50.2 1.4 %shard_map.87 = (f32[2048,128]{1,0:T(8,128)}, f32[2048,128]{1,0:T(8,128)}) custom-call(f32[2048,128]{1,0:T(8,128)S(1)} %get-tuple-element.9.earliest, f32[2048,128]{1,0:T(8,128)S(1)} %get-tuple-element.10.mine, f32[2048,128]{1,0:T(8,128)S(1)} %get-tuple-element.11.theirs, f32[384,128]{1,0:T(8,128)S(1)} %get-tuple-element.12.edge_mine, ...), custom_call_target="tpu_custom_call" | custom-call | tf_op jit(solution)/shard_map/pallas_call | solution.py:583
Async XLA Ops:
  1.3 0.7 %copy-start = (s32[1,128]{1,0:T(1,128)S(1)}, s32[1,128]{1,0:T(1,128)}, u32[]{:S(2)}) copy-start(s32[1,128]{1,0:T(1,128)} %holder_in.1) | copy-start | bytes 1540

commit v6 on v5

--- a/solution.py
+++ b/solution.py
@@ -39,8 +39,8 @@
                 (store, saved),
                 (cond_in, cond_raw),
                 (late_in, late_raw),
-                (cool_in, decay),
-                (heat_in, heat),
+                (cool_in, decay.at[pl.ds(0, cells_x * cells_y)]),
+                (heat_in, heat.at[pl.ds(0, cells_x * cells_y)]),
                 (holder_in, holder),
             ]
         )
@@ -499,10 +499,12 @@
 
 def finish_kernel(sizes, earliest, mine, theirs, edge_mine, edge_theirs, adjoint_out, gradient, total, copy_sem, part_sem):
     cells_x, cells_y = sizes
-    whole = pltpu.make_async_copy(earliest, adjoint_out, copy_sem)
-    whole.start()
     chunk = cells_x // CHUNKS
     copies = []
+    for c in range(CHUNKS):
+        part = pl.ds(c * chunk * cells_y, chunk * cells_y)
+        copies.append(pltpu.make_async_copy(earliest.at[part], adjoint_out.at[part], copy_sem.at[c]))
+        copies[-1].start()
     for c in range(CHUNKS):
         part = pl.ds(c * chunk * cells_y, chunk * cells_y)
         total[part, :] = mine[part, :] + theirs[part, :]
@@ -519,7 +521,6 @@
                 total[here, :] = total[here, :] + (edge_mine[added, :] + edge_theirs[added, :])
         copies.append(pltpu.make_async_copy(total.at[part], gradient.at[part], part_sem.at[c]))
         copies[-1].start()
-    whole.wait()
     for copy in copies:
         copy.wait()
 
@@ -530,8 +531,8 @@
     rows = piece // cells_z
     sizes = (n_tx, n_ty, cells_x, cells_y, cells_z, tiles, rows)
     flat = (cells_x * cells_y, cells_z)
-    faces = ((cells_x + 1) * cells_y, cells_z)
-    padded = (cells_x + 2, 2 * TOP + cells_y, cells_z)
+    roomy = ((cells_x + 2) * cells_y, cells_z)
+    padded = (cells_x + 3, 2 * TOP + cells_y, cells_z)
     edges = (4 * cells_y + 4 * cells_x, cells_z)
     f32 = jnp.float32
 
@@ -550,11 +551,12 @@
             pltpu.SMEM(step_index.shape, jnp.int32),
             pltpu.SMEM(holder.shape, jnp.int32),
             vmem((held, tiles, piece)),
-            vmem(flat),
+            vmem(((tiles + 8) * rows, cells_z)),
             vmem((tiles, rows, cells_z)),
-            *[vmem(flat)] * 4,
+            *[vmem(flat)] * 2,
+            *[vmem(roomy)] * 2,
             *[vmem(padded)] * 5,
-            *[vmem(faces), vmem(padded), vmem(flat)] * 3,
+            *[vmem(roomy), vmem(padded), vmem(roomy)] * 3,
             vmem((10 * cells_y, cells_z)),
             vmem((10 * cells_x, cells_z)),
             vmem((32, cells_z)),
@@ -585,7 +587,7 @@
         out_shape=[shaped(flat, f32)] * 2,
         in_specs=[in_vmem] * 5,
         out_specs=[in_hbm] * 2,
-        scratch_shapes=[vmem(flat), pltpu.SemaphoreType.DMA, pltpu.SemaphoreType.DMA((CHUNKS,))],
+        scratch_shapes=[vmem(roomy), *[pltpu.SemaphoreType.DMA((CHUNKS,))] * 2],
         compiler_params=pltpu.CompilerParams(vmem_limit_bytes=4 << 20),
     )(*results)
     return adjoint_out.reshape(adjoint_in.shape), gradient.reshape(conductivity.shape)

time: 51.6 us -> 51.7 us (level)
  no operation moved by 1% of the time
where the time goes in v6:
time: 51.7 us; the launch traced here: 51.6 us
  Pallas kernels  49.6 us (96%)
  between operations  1.29 us (2%)
  local copies, waits for them, and re-layouts  0.65 us (1%)
    pallas_call x1, Pallas kernels, local(): pl.pallas_call(functools.partial(window_kernel, sizes), out_shape=[shaped...  48.2 us
    pallas_call x1, Pallas kernels, local(): pl.pallas_call(functools.partial(finish_kernel, (cells_x, cells_y)), out_...  1.38 us

profile of v6, /device:TPU:7, one launch (start us, length us, event | category | flops | bytes accessed | tf_op | source)
XLA Modules:
  0.0 51.6 jit_solution(14488953374972404661)
XLA Ops:
  1.3 0.0 copy-start
  1.3 0.6 %copy-done = s32[1,128]{1,0:T(1,128)S(1)} copy-done((s32[1,128]{1,0:T(1,128)S(1)}, s32[1,128]{1,0:T(1,128)}, u32[]{:S(2)}) %copy-start) | copy-done | bytes 536
  1.9 48.2 %shard_map.86 = (f32[2048,128]{1,0:T(8,128)S(1)}, f32[2048,128]{1,0:T(8,128)S(1)}, f32[2048,128]{1,0:T(8,128)S(1)}, f32[384,128]{1,0:T(8,128)S(1)}, f32[384,128]{1,0:T(8,128)S(1)}) custom-call(s32[1]{0:T(128)S(6)} %copy.9.step_in, s32[1,128]{1,0:T(1,128)S(1)} %copy-done, f32[2048,128]{1,0:T(8,128)} %bitcast.8, f32[2048,128]{1,0:T(8,128)} %bitcast.9, ...), custom_call_target="tpu_custom_call" | custom-call | tf_op jit(solution)/shard_map/pallas_call | solution.py:545
  50.2 1.4 %shard_map.87 = (f32[2048,128]{1,0:T(8,128)}, f32[2048,128]{1,0:T(8,128)}) custom-call(f32[2048,128]{1,0:T(8,128)S(1)} %get-tuple-element.9.earliest, f32[2048,128]{1,0:T(8,128)S(1)} %get-tuple-element.10.mine, f32[2048,128]{1,0:T(8,128)S(1)} %get-tuple-element.11.theirs, f32[384,128]{1,0:T(8,128)S(1)} %get-tuple-element.12.edge_mine, ...), custom_call_target="tpu_custom_call" | custom-call | tf_op jit(solution)/shard_map/pallas_call | solution.py:585
Async XLA Ops:
  1.3 0.7 %copy-start = (s32[1,128]{1,0:T(1,128)S(1)}, s32[1,128]{1,0:T(1,128)}, u32[]{:S(2)}) copy-start(s32[1,128]{1,0:T(1,128)} %holder_in.1) | copy-start | bytes 1540
